TPU v7x, 128 devices: a whole 4x4x4 slice. The times are simulated.
128 devices in a mesh: span: 4 (over z_lo, core), xsec: 32 (over y, x, z_hi).
Axes of the slice: x: 4, y: 4, z: 4 (z_hi: 2, z_lo: 2; z = z_hi * 2 + z_lo), core: 2. Of those that a mesh axis runs over, the one named last changes fastest.
Arguments:
- fwd_modes: bfloat16 [3, 32, 8, 9, 9, 512], P(None, 'xsec', None, None, None, 'span'), may hold values from -6 to 6
- adj_modes: bfloat16 [3, 32, 8, 9, 9, 512], P(None, 'xsec', None, None, None, 'span'), may hold values from -6 to 6
- layer_height: float32 [8], replicated, may hold values from 0.5 to 1
- column_width: float32 [32], P('xsec'), may hold values from 0.5 to 1
- wall_mask: int32 [32, 9], P('xsec'), may hold values 0 or 1
Outputs:
- adj_new: bfloat16 [3, 32, 8, 9, 9, 512], P(None, 'xsec', None, None, None, 'span')
- wall_sens: float32 [32, 9, 512], P('xsec', None, 'span')
All inputs are finite; a program needn't handle non-finite values. No bound on the sum of `wall_mask` on one device may be relied on, other than what follows from the above.
Results may differ from a plain program's by a relative error of at most 0.0038.
Values may be sent and summed in bfloat16 or wider, within the bound.
No kernel may reach another device: no remote copies, remote signals or barrier semaphores. Data moves between devices by JAX's collectives and lax.ppermute only.
A program may use at most 192 MiB of HBM per device.

v0:
```python
import functools

import jax
import jax.numpy as jnp
import numpy as np
from jax import lax
from jax.experimental import pallas as pl
from jax.experimental.pallas import tpu as pltpu
from jax.sharding import PartitionSpec as P

NODES = 9
NK = 512
ADV_STEP = 0.0025
DIFFUSE = 5e-05
WALL_GAIN = 0.01
SPAN_GAIN = 1.0 / 32.0
PLANE = NODES * NODES
PAD = 88
ROWS = 3 * 2 * PAD
POINTS = 3 * PLANE * 8
COLS = 3 * NODES
F32 = jnp.float32
BF16 = jnp.bfloat16
MIB = 1 << 20


def cheb_table(number):
    degree = number - 1
    points = -np.cos(np.pi * np.arange(number) / degree)
    factor = np.where((np.arange(number) == 0) | (np.arange(number) == degree), 2.0, 1.0)
    parity = (-1.0) ** np.arange(number)
    spacing = points[:, None] - points[None, :] + np.eye(number)
    matrix = factor[:, None] * parity[:, None] * parity[None, :] / (factor[None, :] * spacing)
    matrix = matrix * (1.0 - np.eye(number))
    matrix = matrix - np.eye(number) * np.sum(matrix, axis=1)[:, None]
    return matrix.astype(np.float32)


def span_tables(modes):
    indices = np.arange(modes)
    pair_index = indices // 2
    wavenum = np.where(indices == 1, modes // 2, pair_index)
    planes = np.arange(modes)
    phases = 2.0 * np.pi * (wavenum[:, None] * planes[None, :] % modes) / modes
    basis_rows = np.where((indices % 2 == 0)[:, None], np.cos(phases), np.sin(phases))
    basis_rows = np.where((indices <= 1)[:, None], np.cos(phases), basis_rows)
    norm_gain = 1.0 / np.sqrt(modes / 2.0)
    weights_k = np.where(indices <= 1, 1.0, 2.0)
    synthesis = (basis_rows * norm_gain).astype(np.float32)
    analysis = ((basis_rows * (weights_k / (modes * norm_gain))[:, None]).T).astype(np.float32)
    slopes = np.where(indices <= 1, 0.0, pair_index * SPAN_GAIN).astype(np.float32)
    kappa_sq = ((wavenum * SPAN_GAIN) ** 2).astype(np.float32)
    return synthesis, analysis, slopes, kappa_sq


def halves(table):
    high = table.astype(jnp.bfloat16)
    return high, (table.astype(np.float64) - high.astype(np.float64)).astype(jnp.bfloat16)


DERIV = cheb_table(NODES).astype(np.float64)
INNER = DERIV[:, 1:8] @ DERIV[1:8, :]
FACED = INNER + 0.5 * np.outer(DERIV[:, 0], DERIV[0]) + 0.5 * np.outer(DERIV[:, 8], DERIV[8])


def plane_tables():
    synthesis, analysis, slopes, kappa_sq = span_tables(NK)
    wave = np.zeros((NK, NK))
    wave[1::2] = slopes[0::2, None].astype(np.float64) * synthesis[0::2]
    wave[0::2] = -slopes[1::2, None].astype(np.float64) * synthesis[1::2]
    radial = np.kron(DERIV, np.eye(NODES))
    around = np.kron(np.eye(NODES), DERIV)
    both = np.zeros((2, 2, PAD, 2, PAD))
    for layer in range(2):
        both[0, layer, :PLANE, layer, :PLANE] = radial
        both[1, layer, :PLANE, layer, :PLANE] = around
    high, low = halves(both.reshape(4 * PAD, 2 * PAD))
    slope = np.concatenate([high, low, high], axis=1)
    kappa = np.broadcast_to(kappa_sq.reshape(4, 1, 128), (4, 8, 128)).astype(np.float32)
    return synthesis.astype(jnp.bfloat16), halves(wave), slope, halves(analysis), kappa


def smem():
    return pl.BlockSpec(memory_space=pltpu.SMEM)


def vmem():
    return pl.BlockSpec(memory_space=pltpu.VMEM)


def call(kernel, name, outs, scratch, specs, flops, nbytes):
    return pl.pallas_call(
        kernel,
        out_shape=[jax.ShapeDtypeStruct(shape, kind) for shape, kind in outs],
        in_specs=specs,
        out_specs=[vmem() for _ in outs],
        scratch_shapes=scratch,
        compiler_params=pltpu.CompilerParams(vmem_limit_bytes=40 * MIB),
        cost_estimate=pl.CostEstimate(flops=flops, bytes_accessed=nbytes, transcendentals=0),
        name=name,
    )


def repack_kernel(pos_ref, x_ref, *refs):
    outs, wide = refs[:4], refs[4]
    pos = pos_ref[0]
    wide[pl.ds(0, POINTS), :] = x_ref[...].astype(F32)
    keep = lax.broadcasted_iota(jnp.int32, (PAD, 128), 0) < PLANE
    for flip, out in enumerate(outs):
        group = pos ^ flip
        for comp in range(3):
            parts = []
            for layer in range(2):
                start = comp * PLANE * 8 + 2 * group + layer
                rows = wide[pl.ds(start, PAD, stride=8), :]
                parts.append(jnp.where(keep, rows, 0.0))
            block = jnp.concatenate(parts, axis=0).astype(BF16)
            out[comp * 2 * PAD : (comp + 1) * 2 * PAD, :] = block


def repack(pos, field, name):
    return call(
        repack_kernel,
        name,
        [((ROWS, 128), BF16)] * 4,
        [pltpu.VMEM((POINTS + 56, 128), F32)],
        [smem(), vmem()],
        1_000_000,
        1_000_000,
    )(pos, field)


def force_kernel(
    pos_ref, height_ref, width_ref, *refs
):
    fwd, adj = refs[0:4], refs[4:8]
    synth_ref, wave_hi_ref, wave_lo_ref, slope_ref, an_hi_ref, an_lo_ref = refs[8:14]
    outs = refs[14:18]
    planes, zplanes, grads, force = refs[18:22]
    pos = pos_ref[0]

    def gather(ref):
        parts = [ref[pl.ds(pl.multiple_of(128 * (pos ^ flip), 128), 128), :] for flip in range(4)]
        return jnp.concatenate(parts, axis=0)

    synth, wave_hi, wave_lo = gather(synth_ref), gather(wave_hi_ref), gather(wave_lo_ref)
    slope = slope_ref[...]
    for which, chunks in ((0, fwd), (1, adj)):
        modes = jnp.concatenate([chunk[...] for chunk in chunks], axis=1)
        planes[which] = jnp.dot(modes, synth, preferred_element_type=F32)
        zplanes[which] = jnp.dot(modes, wave_hi, preferred_element_type=F32) + jnp.dot(
            modes, wave_lo, preferred_element_type=F32
        )
        for comp in range(3):
            block = planes[which, comp * 2 * PAD : (comp + 1) * 2 * PAD, :]
            high = block.astype(BF16)
            low = (block - high.astype(F32)).astype(BF16)
            stack = jnp.concatenate([high, high, low], axis=0)
            grads[which, comp] = jnp.dot(slope, stack, preferred_element_type=F32)

    across = 2.0 / jnp.full((8, 128), width_ref[0], F32)
    for layer in range(2):
        along = 2.0 / jnp.full((8, 128), height_ref[2 * pos + layer], F32)
        for tile in range(PAD // 8):
            row = layer * PAD + 8 * tile
            for lane in range(0, NK, 128):
                lanes = slice(lane, lane + 128)

                def plane(which, comp):
                    at = comp * 2 * PAD + row
                    return planes[which, at : at + 8, lanes]

                def zplane(which, comp):
                    at = comp * 2 * PAD + row
                    return zplanes[which, at : at + 8, lanes]

                def grad(which, direc, comp):
                    at = direc * 2 * PAD + row
                    return grads[which, comp, at : at + 8, lanes]

                fwd_r = plane(0, 0) * along
                fwd_t = plane(0, 1) * across
                fwd_z = plane(0, 2)
                adj_p = [plane(1, comp) for comp in range(3)]
                pulled = [
                    along * sum(adj_p[comp] * grad(0, 0, comp) for comp in range(3)),
                    across * sum(adj_p[comp] * grad(0, 1, comp) for comp in range(3)),
                    sum(adj_p[comp] * zplane(0, comp) for comp in range(3)),
                ]
                for comp in range(3):
                    carried = (
                        fwd_r * grad(1, 0, comp) + fwd_t * grad(1, 1, comp) + fwd_z * zplane(1, comp)
                    )
                    at = comp * 2 * PAD + row
                    force[at : at + 8, lanes] = carried - pulled[comp]

    def pick(ref):
        return jnp.concatenate([ref[pos ^ flip] for flip in range(4)], axis=1)

    an_hi, an_lo = pick(an_hi_ref), pick(an_lo_ref)
    total = force[...]
    high = total.astype(BF16)
    low = (total - high.astype(F32)).astype(BF16)
    result = (
        jnp.dot(high, an_hi, preferred_element_type=F32)
        + jnp.dot(low, an_hi, preferred_element_type=F32)
        + jnp.dot(high, an_lo, preferred_element_type=F32)
    ).astype(BF16)
    for flip, out in enumerate(outs):
        out[...] = result[:, 128 * flip : 128 * (flip + 1)]


def forcing(pos, heights, widths, fwd, adj, tables):
    synth, (wave_hi, wave_lo), slope, (an_hi, an_lo) = tables
    split = lambda table: jnp.asarray(table.reshape(NK, 4, 128).transpose(1, 0, 2))
    constants = [
        jnp.asarray(synth),
        jnp.asarray(wave_hi),
        jnp.asarray(wave_lo),
        jnp.asarray(slope),
        split(an_hi),
        split(an_lo),
    ]
    return call(
        force_kernel,
        "adjoint_forcing",
        [((ROWS, 128), BF16)] * 4,
        [
            pltpu.VMEM((2, ROWS, NK), F32),
            pltpu.VMEM((2, ROWS, NK), F32),
            pltpu.VMEM((2, 3, 4 * PAD, NK), F32),
            pltpu.VMEM((ROWS, NK), F32),
        ],
        [smem(), smem(), smem()] + [vmem()] * 14,
        5_000_000_000,
        8_000_000,
    )(pos, heights, widths, *fwd, *adj, *constants)


def mirror(matrix):
    even = np.concatenate(
        [0.5 * (matrix[:5, :4] + matrix[:5, :4:-1]), matrix[:5, 4:5]], axis=1
    )
    odd = 0.5 * (matrix[:4, :4] - matrix[:4, :4:-1])
    return even, odd


def weighted(coeffs, values):
    total = None
    for coeff, value in zip(coeffs, values):
        term = float(coeff) * value
        total = term if total is None else total + term
    return total


def parity(values):
    even = [values[n] + values[8 - n] for n in range(4)] + [values[4]]
    odd = [values[n] - values[8 - n] for n in range(4)]
    return even, odd


def ends(even, odd):
    row_even = np.concatenate([0.5 * (DERIV[0, :4] + DERIV[0, :4:-1]), DERIV[0, 4:5]])
    row_odd = 0.5 * (DERIV[0, :4] - DERIV[0, :4:-1])
    first, second = weighted(row_even, even), weighted(row_odd, odd)
    return second + first, second - first


def unfold(even, odd):
    low = [even[n] + odd[n] for n in range(4)]
    high = [even[n] - odd[n] for n in range(4)]
    return low + [even[4]] + high[::-1]


def layer_vectors(height_ref):
    layer = lax.broadcasted_iota(jnp.int32, (8, 128), 0)
    height = jnp.full((8, 128), height_ref[0], F32)
    for index in range(1, 8):
        height = jnp.where(layer == index, height_ref[index], height)
    along = 2.0 / height
    below = pltpu.roll(along, 1, 0)
    above = pltpu.roll(along, 7, 0)
    bottom, top = layer == 0, layer == 7
    own_low = jnp.where(bottom, 1.0, 0.5)
    own_high = jnp.where(top, 1.0, 0.5)
    from_below = jnp.where(bottom, 0.0, 0.5)
    from_above = jnp.where(top, 0.0, 0.5)
    return dict(
        layer=layer,
        along=along,
        own_low=own_low,
        own_high=own_high,
        from_below=from_below,
        from_above=from_above,
        grad_below=from_below * below / along,
        grad_above=from_above * above / along,
    )


def local_step(vec, width, kappa, load, store, sent, two_away, visc, faces):
    across = 2.0 / jnp.full((8, 128), width, F32)
    scale_t = DIFFUSE * across * across
    scale_r = DIFFUSE * vec["along"] * vec["along"]
    scale_k = DIFFUSE * kappa
    even_t, odd_t = mirror(FACED)
    even_r, odd_r = mirror(INNER)
    mix_even = 0.5 * (DERIV[:5, 0] - DERIV[:5, 8])
    mix_odd = 0.5 * (DERIV[:4, 0] + DERIV[:4, 8])

    def shared(low, high):
        low_new = vec["own_low"] * low + vec["from_below"] * pltpu.roll(high, 1, 0)
        high_new = vec["own_high"] * high + vec["from_above"] * pltpu.roll(low, 7, 0)
        return low_new, high_new

    right_ref, left_ref = sent
    right_far, left_far = two_away

    for comp in range(3):
        edge_low, edge_high = [], []
        for i in range(NODES):
            values = [load(comp, i, j) for j in range(NODES)]
            even, odd = parity(values)
            low, high = ends(even, odd)
            edge_low.append(across * low)
            edge_high.append(across * high)
            even_out = [weighted(even_t[n], even) for n in range(5)]
            odd_out = [weighted(odd_t[n], odd) for n in range(4)]
            for j, value in enumerate(unfold(even_out, odd_out)):
                visc[pl.ds(8 * (i * NODES + j), 8), :] = scale_t * value
        for edge, ref in ((edge_low, 0), (edge_high, 1)):
            edge[0], edge[8] = shared(edge[0], edge[8])
            for i in range(NODES):
                faces[pl.ds(8 * ((ref * 3 + comp) * NODES + i), 8), :] = edge[i]
        for j in range(NODES):
            values = [load(comp, i, j) for i in range(NODES)]
            even, odd = parity(values)
            low, high = ends(even, odd)
            low_mean = vec["own_low"] * low + vec["grad_below"] * pltpu.roll(high, 1, 0)
            high_mean = vec["own_high"] * high + vec["grad_above"] * pltpu.roll(low, 7, 0)
            differ, total = low_mean - high_mean, low_mean + high_mean
            even_out = [
                weighted(even_r[n], even) + float(mix_even[n]) * differ for n in range(5)
            ]
            odd_out = [weighted(odd_r[n], odd) + float(mix_odd[n]) * total for n in range(4)]
            lap = [
                scale_r * value - scale_k * values[i] + visc[pl.ds(8 * (i * NODES + j), 8), :]
                for i, value in enumerate(unfold(even_out, odd_out))
            ]
            lap[0], lap[8] = shared(lap[0], lap[8])
            if j == 0 or j == 8:
                ref, side = (left_ref, 0) if j == 0 else (right_ref, 1)
                for i in range(NODES):
                    edge = faces[pl.ds(8 * ((side * 3 + comp) * NODES + i), 8), :]
                    pair = jnp.concatenate([edge, lap[i]], axis=0).astype(BF16)
                    ref[pl.ds(16 * (comp * NODES + i), 16), :] = pair
            for i in range(NODES):
                step = 0.5 * lap[i] if j == 0 or j == 8 else lap[i]
                store(comp, i, j, values[i], step)
    for side, ref in ((0, left_far), (1, right_far)):
        for block in range(14):
            first = faces[pl.ds(8 * (side * COLS + 2 * block), 8), :]
            if 2 * block + 1 < COLS:
                second = faces[pl.ds(8 * (side * COLS + 2 * block + 1), 8), :]
            else:
                second = jnp.zeros((8, 128), F32)
            ref[pl.ds(16 * block, 16), :] = jnp.concatenate([first, second], axis=0).astype(BF16)
    return across


def spot(comp, i, j):
    return pl.ds(8 * ((comp * NODES + i) * NODES + j), 8)


def first_kernel(pos_ref, height_ref, width_ref, kappa_ref, x_ref, *refs):
    out, right, left, right_far, left_far, wide, visc, faces = refs
    wide[...] = x_ref[...].astype(F32)

    def load(comp, i, j):
        return wide[spot(comp, i, j), :]

    def store(comp, i, j, value, step):
        out[spot(comp, i, j), :] = value + step

    vec = layer_vectors(height_ref)
    kappa = kappa_ref[pos_ref[0]]
    across = local_step(
        vec, width_ref[0], kappa, load, store, (right, left), (right_far, left_far), visc, faces
    )
    high = across.astype(BF16).astype(F32)
    mid = (across - high).astype(BF16).astype(F32)
    low = across - high - mid
    layer = vec["layer"]
    note = jnp.where(layer == 0, high, jnp.where(layer == 1, mid, jnp.where(layer == 2, low, 0.0)))
    block = jnp.concatenate([note, jnp.zeros((8, 128), F32)], axis=0).astype(BF16)
    for ref in (right, left):
        ref[pl.ds(16 * COLS, 16), :] = block


def second_kernel(pos_ref, height_ref, width_ref, kappa_ref, base_ref, *refs):
    chunks = refs[:4]
    out, right, left, right_far, left_far, push, wide, visc, faces = refs[4:]
    pos = pos_ref[0]
    for flip, chunk in enumerate(chunks):
        group = pos ^ flip
        for comp in range(3):
            block = ADV_STEP * chunk[comp * 2 * PAD : (comp + 1) * 2 * PAD, :].astype(F32)
            for layer in range(2):
                start = comp * PLANE * 8 + 2 * group + layer
                push[pl.ds(start, PLANE, stride=8), :] = block[layer * PAD : layer * PAD + PLANE]
    vec = layer_vectors(height_ref)
    off_wall = jnp.where(vec["layer"] == 0, 0.0, 1.0)
    for comp in range(3):
        for i in range(NODES):
            for j in range(NODES):
                at = spot(comp, i, j)
                value = base_ref[at, :] + push[at, :]
                wide[at, :] = value * off_wall if i == 0 else value

    def load(comp, i, j):
        return wide[spot(comp, i, j), :]

    def store(comp, i, j, value, step):
        at = spot(comp, i, j)
        out[at, :] = value + push[at, :] + step

    local_step(
        vec,
        width_ref[0],
        kappa_ref[pos],
        load,
        store,
        (right, left),
        (right_far, left_far),
        visc,
        faces,
    )


def join_step(width, near, far, own, sides, state, store):
    from_left, from_right = near
    far_left, far_right = far
    own_right, own_left = own
    across = 2.0 / jnp.full((8, 128), width, F32)
    gain = (0.5 * DIFFUSE) * across
    gain_left, gain_right = (0.5 * DIFFUSE) * sides[0], (0.5 * DIFFUSE) * sides[1]
    for block in range(14):
        far_l = far_left[pl.ds(16 * block, 16), :].astype(F32)
        far_r = far_right[pl.ds(16 * block, 16), :].astype(F32)
        for half in range(2):
            col = 2 * block + half
            if col >= COLS:
                continue
            comp, i = divmod(col, NODES)
            at = pl.ds(16 * col, 16)
            pair_l, pair_r = from_left[at, :].astype(F32), from_right[at, :].astype(F32)
            mine_low = own_left[at, :].astype(F32)[0:8]
            mine_high = own_right[at, :].astype(F32)[0:8]
            grad_l, grad_r = gain * pair_l[0:8], gain * pair_r[0:8]
            two_l, two_r = far_l[8 * half : 8 * half + 8], far_r[8 * half : 8 * half + 8]
            for j in range(NODES):
                add = float(DERIV[j, 0]) * grad_l + float(DERIV[j, 8]) * grad_r
                if j == 0:
                    other = gain_left * (float(DERIV[8, 0]) * two_l + float(DERIV[8, 8]) * mine_low)
                    add = 0.5 * (add + pair_l[8:16] + other)
                if j == 8:
                    other = gain_right * (float(DERIV[0, 0]) * mine_high + float(DERIV[0, 8]) * two_r)
                    add = 0.5 * (add + pair_r[8:16] + other)
                store(comp, i, j, state[spot(comp, i, j), :] + add)


def first_join_kernel(width_ref, *refs):
    near, far, own = refs[0:2], refs[2:4], refs[4:6]
    state, out, sides_out = refs[6:9]
    sides = []
    for side, ref in enumerate(near):
        note = ref[pl.ds(16 * COLS, 16), :].astype(F32)[0:8]
        value = jnp.broadcast_to(jnp.sum(note, axis=0, keepdims=True), (8, 128))
        sides_out[pl.ds(8 * side, 8), :] = value
        sides.append(value)

    def store(comp, i, j, value):
        out[spot(comp, i, j), :] = value

    join_step(width_ref[0], near, far, own, sides, state, store)


def second_join_kernel(width_ref, height_ref, mask_ref, *refs):
    near, far, own = refs[0:2], refs[2:4], refs[4:6]
    sides_ref, state, out, wall, full = refs[6:11]
    sides = [sides_ref[pl.ds(0, 8), :], sides_ref[pl.ds(8, 8), :]]
    layer = lax.broadcasted_iota(jnp.int32, (8, 128), 0)
    off_wall = jnp.where(layer == 0, 0.0, 1.0)

    def store(comp, i, j, value):
        full[spot(comp, i, j), :] = value * off_wall if i == 0 else value

    join_step(width_ref[0], near, far, own, sides, state, store)
    out[...] = full[...].astype(BF16)
    along = 2.0 / jnp.full((8, 128), height_ref[0], F32)
    for j in range(NODES):
        rows = weighted(DERIV[0], [full[spot(0, i, j), :] for i in range(NODES)])
        rows = (WALL_GAIN * along) * rows * mask_ref[0, j].astype(F32)
        wall[pl.ds(j, 1), :] = rows[0:1]


def ring(value, shift):
    count = lax.axis_size("xsec")
    return lax.ppermute(value, "xsec", [(n, (n + shift) % count) for n in range(count)])


def swap(value, flip):
    return lax.ppermute(value, "span", [(n, n ^ flip) for n in range(lax.axis_size("span"))])


def halo(right, left, right_far, left_far):
    from_left, from_right = ring(right, 1), ring(left, -1)
    far_left, far_right = ring(right_far, 2), ring(left_far, -2)
    return from_left, from_right, far_left, far_right


def local(fwd_modes, adj_modes, layer_height, column_width, wall_mask):
    synth, wave, slope, analysis, kappa = plane_tables()
    kappa = jnp.asarray(kappa)
    pos = lax.axis_index("span").astype(jnp.int32).reshape(1)

    def resident(field):
        return field.transpose(0, 1, 3, 4, 2, 5).reshape(POINTS, 128)

    fwd_flat, adj_flat = resident(fwd_modes), resident(adj_modes)
    state_shapes = [((POINTS, 128), F32)]
    far_shapes = [((224, 128), BF16)] * 2
    work = [
        pltpu.VMEM((POINTS, 128), F32),
        pltpu.VMEM((PLANE * 8, 128), F32),
        pltpu.VMEM((2 * COLS * 8, 128), F32),
    ]

    adj_own, *adj_away = repack(pos, adj_flat, "adj_groups")
    adj_all = [adj_own] + [swap(part, flip + 1) for flip, part in enumerate(adj_away)]
    fwd_own, *fwd_away = repack(pos, fwd_flat, "fwd_groups")
    fwd_all = [fwd_own] + [swap(part, flip + 1) for flip, part in enumerate(fwd_away)]

    state, right, left, right_far, left_far = call(
        first_kernel,
        "first_substep",
        state_shapes + [((16 * COLS + 16, 128), BF16)] * 2 + far_shapes,
        work,
        [smem(), smem(), smem(), vmem(), vmem()],
        50_000_000,
        3_000_000,
    )(pos, layer_height, column_width, kappa, adj_flat)
    got = halo(right, left, right_far, left_far)

    parts = forcing(
        pos, layer_height, column_width, fwd_all, adj_all, (synth, wave, slope, analysis)
    )
    parts = [parts[0]] + [swap(part, flip + 1) for flip, part in enumerate(parts[1:])]

    base, sides = call(
        first_join_kernel,
        "first_join",
        state_shapes + [((16, 128), F32)],
        [],
        [smem()] + [vmem()] * 7,
        10_000_000,
        3_000_000,
    )(column_width, *got, right, left, state)

    state, right, left, right_far, left_far = call(
        second_kernel,
        "second_substep",
        state_shapes + [((16 * COLS, 128), BF16)] * 2 + far_shapes,
        [pltpu.VMEM((POINTS, 128), F32)] + work,
        [smem(), smem(), smem()] + [vmem()] * 6,
        50_000_000,
        4_000_000,
    )(pos, layer_height, column_width, kappa, base, *parts)
    got = halo(right, left, right_far, left_far)

    adj_new, wall = call(
        second_join_kernel,
        "second_join",
        [((POINTS, 128), BF16), ((NODES, 128), F32)],
        [pltpu.VMEM((POINTS, 128), F32)],
        [smem()] * 3 + [vmem()] * 8,
        10_000_000,
        3_000_000,
    )(column_width, layer_height, wall_mask, *got, right, left, sides, state)
    adj_new = adj_new.reshape(3, 1, NODES, NODES, 8, 128).transpose(0, 1, 4, 2, 3, 5)
    return adj_new, wall.reshape(1, NODES, 128)


def solution(mesh):
    return jax.shard_map(
        local,
        mesh=mesh,
        in_specs=(
            P(None, "xsec", None, None, None, "span"),
            P(None, "xsec", None, None, None, "span"),
            P(),
            P("xsec"),
            P("xsec", None),
        ),
        out_specs=(P(None, "xsec", None, None, None, "span"), P("xsec", None, "span")),
        check_vma=False,
    )
```

profile of v0, /device:TPU:30, one launch (start us, length us, event | category | flops | bytes accessed | tf_op | source)
XLA Modules:
  0.0 63.9 jit_solution(2525299643752827439)
XLA Ops:
  0.6 0.0 copy-start
  0.6 1.0 %copy-done = bf16[3,1,8,9,9,128]{5,2,4,3,1,0:T(8,128)(2,1)S(1)} copy-done((bf16[3,1,8,9,9,128]{5,2,4,3,1,0:T(8,128)(2,1)S(1)}, bf16[3,1,8,9,9,128]{5,2,4,3,1,0:T(8,128)(2,1)}, u32[]{:S(2)}) %copy-start) | copy-done | bytes 497688
  1.7 0.0 copy-start.1
  1.7 0.2 adj_groups.1
  1.9 0.1 collective-permute-start.7
  2.0 2.0 %collective-permute-start.8 = (bf16[528,128]{1,0:T(8,128)(2,1)S(1)}, bf16[528,128]{1,0:T(8,128)(2,1)S(1)}, u32[]{:S(2)}, u32[]{:S(2)}) collective-permute-start(bf16[528,128]{1,0:T(8,128)(2,1)S(1)} %get-tuple-element.40), channel_id=1, source_target_pairs={{0,64},{32,96},{64,0},{96,32},{1,65},{33,97},{65,1},{97,33},{2,66}... | collective-permute-start | bytes 405512 | tf_op jit(solution)/shard_map/ppermute | solution.py:512
  4.0 0.1 collective-permute-start.9
  4.1 0.0 copy-start.2
  4.1 1.0 %copy-done.2 = bf16[3,1,8,9,9,128]{5,2,4,3,1,0:T(8,128)(2,1)S(1)} copy-done((bf16[3,1,8,9,9,128]{5,2,4,3,1,0:T(8,128)(2,1)S(1)}, bf16[3,1,8,9,9,128]{5,2,4,3,1,0:T(8,128)(2,1)}, u32[]{:S(2)}) %copy-start.2) | copy-done | bytes 497688
  5.1 0.0 copy-start.3
  5.1 0.0 copy-start.11
  5.1 0.2 fwd_groups.1
  5.3 0.2 collective-permute-start.4
  5.6 1.9 %collective-permute-start.5 = (bf16[528,128]{1,0:T(8,128)(2,1)S(1)}, bf16[528,128]{1,0:T(8,128)(2,1)S(1)}, u32[]{:S(2)}, u32[]{:S(2)}) collective-permute-start(bf16[528,128]{1,0:T(8,128)(2,1)S(1)} %get-tuple-element.36), channel_id=1, source_target_pairs={{0,64},{32,96},{64,0},{96,32},{1,65},{33,97},{65,1},{97,33},{2,66}... | collective-permute-start | bytes 405512 | tf_op jit(solution)/shard_map/ppermute | solution.py:512
  7.5 0.0 collective-permute-done.7.refs_5_
  7.5 0.0 copy-start.4
  7.5 0.0 copy-start.6
  7.5 0.0 collective-permute-start.6
  8.2 0.0 copy-done.1
  8.2 0.0 copy-done.3
  8.2 0.0 copy-done.4
  8.3 1.8 %first_substep.1 = (f32[1944,128]{1,0:T(8,128)S(1)}, bf16[448,128]{1,0:T(8,128)(2,1)S(1)}, bf16[448,128]{1,0:T(8,128)(2,1)S(1)}, bf16[224,128]{1,0:T(8,128)(2,1)S(1)}, bf16[224,128]{1,0:T(8,128)(2,1)S(1)}) custom-call(s32[1]{0:T(128)} %bitcast.pos_ref, f32[8]{0:T(128)S(1)} %copy-done.4, f32[1]{0:T(128)S(6)} %copy.16.width_ref, f32[4,8,128]{2,1,0:T(8,128)S(1)} %copy-done.3, ...), custom_call_target="tpu_custom_call" | custom-call | flops 50000000 | bytes 3000000 | tf_op jit(solution)/shard_map/first_substep/pallas_call | solution.py:543
  10.0 0.0 collective-permute-done.8.refs_6_
  10.0 0.2 collective-permute-start.2
  10.2 0.6 collective-permute-done.9.refs_7_
  10.8 1.3 %collective-permute-start.3 = (bf16[224,128]{1,0:T(8,128)(2,1)S(1)}, bf16[224,128]{1,0:T(8,128)(2,1)S(1)}, u32[]{:S(2)}, u32[]{:S(2)}) collective-permute-start(bf16[224,128]{1,0:T(8,128)(2,1)S(1)} %get-tuple-element.31), channel_id=1, source_target_pairs={{0,30},{1,31},{2,0},{3,1},{4,2},{5,3},{6,4},{7,5},{8,6},{9,7},{10,... | collective-permute-start | bytes 172040 | tf_op jit(solution)/shard_map/ppermute | solution.py:508
  12.1 0.0 collective-permute-done.4.refs_1_
  12.1 2.1 %collective-permute-done.5.refs_2_ = bf16[528,128]{1,0:T(8,128)(2,1)S(1)} collective-permute-done((bf16[528,128]{1,0:T(8,128)(2,1)S(1)}, bf16[528,128]{1,0:T(8,128)(2,1)S(1)}, u32[]{:S(2)}, u32[]{:S(2)}) %collective-permute-start.5) | collective-permute-done | bytes 135200 | tf_op jit(solution)/shard_map/ppermute | solution.py:512
  14.2 2.3 %collective-permute-done.6.refs_3_ = bf16[528,128]{1,0:T(8,128)(2,1)S(1)} collective-permute-done((bf16[528,128]{1,0:T(8,128)(2,1)S(1)}, bf16[528,128]{1,0:T(8,128)(2,1)S(1)}, u32[]{:S(2)}, u32[]{:S(2)}) %collective-permute-start.6) | collective-permute-done | bytes 135200 | tf_op jit(solution)/shard_map/ppermute | solution.py:512
  16.6 0.0 copy-done.11
  16.6 0.0 copy-done.6
  16.6 0.0 copy-start.7
  16.6 1.0 %copy-done.7 = bf16[512,512]{1,0:T(8,128)(2,1)S(1)} copy-done((bf16[512,512]{1,0:T(8,128)(2,1)S(1)}, bf16[512,512]{1,0:T(8,128)(2,1)}, u32[]{:S(2)}) %copy-start.7) | copy-done | bytes 524312
  17.6 0.0 copy-start.8
  17.6 1.0 %copy-done.8 = bf16[512,512]{1,0:T(8,128)(2,1)S(1)} copy-done((bf16[512,512]{1,0:T(8,128)(2,1)S(1)}, bf16[512,512]{1,0:T(8,128)(2,1)}, u32[]{:S(2)}) %copy-start.8) | copy-done | bytes 524312
  18.6 0.0 copy-start.9
  18.7 1.0 %copy-done.9 = bf16[4,512,128]{2,1,0:T(8,128)(2,1)S(1)} copy-done((bf16[4,512,128]{2,1,0:T(8,128)(2,1)S(1)}, bf16[4,512,128]{2,1,0:T(8,128)(2,1)}, u32[]{:S(2)}) %copy-start.9) | copy-done | bytes 524312
  19.7 1.0 %copy-done.10 = bf16[4,512,128]{2,1,0:T(8,128)(2,1)S(1)} copy-done((bf16[4,512,128]{2,1,0:T(8,128)(2,1)S(1)}, bf16[4,512,128]{2,1,0:T(8,128)(2,1)}, u32[]{:S(2)}) %copy-start.10) | copy-done | bytes 524312
  20.7 5.3 %adjoint_forcing.1 = (bf16[528,128]{1,0:T(8,128)(2,1)S(1)}, bf16[528,128]{1,0:T(8,128)(2,1)S(1)}, bf16[528,128]{1,0:T(8,128)(2,1)S(1)}, bf16[528,128]{1,0:T(8,128)(2,1)S(1)}) custom-call(s32[1]{0:T(128)} %bitcast.pos_ref, f32[8]{0:T(128)S(1)} %copy-done.4, f32[1]{0:T(128)S(6)} %copy.16.width_ref, bf16[528,128]{1,0:T(8,128)(2,1)S(1)} %get-tuple-element.34.refs_0_, ...), custom_call_target="tpu_custom_call" | custom-call | flops 5000000000 | bytes 8000000 | tf_op jit(solution)/shard_map/adjoint_forcing/pallas_call | solution.py:224
  26.0 0.5 collective-permute-start.10
  26.5 1.8 %collective-permute-start.11 = (bf16[528,128]{1,0:T(8,128)(2,1)S(1)}, bf16[528,128]{1,0:T(8,128)(2,1)S(1)}, u32[]{:S(2)}, u32[]{:S(2)}) collective-permute-start(bf16[528,128]{1,0:T(8,128)(2,1)S(1)} %get-tuple-element.44), channel_id=1, source_target_pairs={{0,64},{32,96},{64,0},{96,32},{1,65},{33,97},{65,1},{97,33},{2,66}... | collective-permute-start | bytes 405512 | tf_op jit(solution)/shard_map/ppermute | solution.py:512
  28.3 0.0 collective-permute-start.12
  28.3 0.0 collective-permute-done.2.refs_2_
  28.3 3.6 %collective-permute-start = (bf16[448,128]{1,0:T(8,128)(2,1)S(1)}, bf16[448,128]{1,0:T(8,128)(2,1)S(1)}, u32[]{:S(2)}, u32[]{:S(2)}) collective-permute-start(bf16[448,128]{1,0:T(8,128)(2,1)S(1)} %get-tuple-element.28.refs_4_), channel_id=1, source_target_pairs={{0,1},{1,2},{2,3},{3,4},{4,5},{5,6},{6,7},{7,8},{8,9},{9,10},{10,1... | collective-permute-start | bytes 344072 | tf_op jit(solution)/shard_map/ppermute | solution.py:508
  31.9 0.0 collective-permute-done.3.refs_3_
  31.9 0.9 %collective-permute-start.1 = (bf16[448,128]{1,0:T(8,128)(2,1)S(1)}, bf16[448,128]{1,0:T(8,128)(2,1)S(1)}, u32[]{:S(2)}, u32[]{:S(2)}) collective-permute-start(bf16[448,128]{1,0:T(8,128)(2,1)S(1)} %get-tuple-element.29.refs_5_), channel_id=1, source_target_pairs={{0,31},{1,0},{2,1},{3,2},{4,3},{5,4},{6,5},{7,6},{8,7},{9,8},{10,9... | collective-permute-start | bytes 344072 | tf_op jit(solution)/shard_map/ppermute | solution.py:508
  32.7 4.0 %collective-permute-done.refs_0_ = bf16[448,128]{1,0:T(8,128)(2,1)S(1)} collective-permute-done((bf16[448,128]{1,0:T(8,128)(2,1)S(1)}, bf16[448,128]{1,0:T(8,128)(2,1)S(1)}, u32[]{:S(2)}, u32[]{:S(2)}) %collective-permute-start) | collective-permute-done | bytes 114720 | tf_op jit(solution)/shard_map/ppermute | solution.py:508
  36.7 6.5 %collective-permute-done.1.refs_1_ = bf16[448,128]{1,0:T(8,128)(2,1)S(1)} collective-permute-done((bf16[448,128]{1,0:T(8,128)(2,1)S(1)}, bf16[448,128]{1,0:T(8,128)(2,1)S(1)}, u32[]{:S(2)}, u32[]{:S(2)}) %collective-permute-start.1) | collective-permute-done | bytes 114720 | tf_op jit(solution)/shard_map/ppermute | solution.py:508
  43.2 0.2 first_join.1
  43.5 0.0 collective-permute-done.10.refs_1_
  43.5 0.0 collective-permute-done.11.refs_2_
  43.5 0.0 collective-permute-done.12.refs_3_
  43.5 2.1 %second_substep.1 = (f32[1944,128]{1,0:T(8,128)S(1)}, bf16[432,128]{1,0:T(8,128)(2,1)S(1)}, bf16[432,128]{1,0:T(8,128)(2,1)S(1)}, bf16[224,128]{1,0:T(8,128)(2,1)S(1)}, bf16[224,128]{1,0:T(8,128)(2,1)S(1)}) custom-call(s32[1]{0:T(128)} %bitcast.pos_ref, f32[8]{0:T(128)S(1)} %copy-done.4, f32[1]{0:T(128)S(6)} %copy.16.width_ref, f32[4,8,128]{2,1,0:T(8,128)S(1)} %copy-done.3, ...), custom_call_target="tpu_custom_call" | custom-call | flops 50000000 | bytes 4000000 | tf_op jit(solution)/shard_map/second_substep/pallas_call | solution.py:569
  45.6 0.1 collective-permute-start.13
  45.7 4.4 %collective-permute-start.14 = (bf16[432,128]{1,0:T(8,128)(2,1)S(1)}, bf16[432,128]{1,0:T(8,128)(2,1)S(1)}, u32[]{:S(2)}, u32[]{:S(2)}) collective-permute-start(bf16[432,128]{1,0:T(8,128)(2,1)S(1)} %get-tuple-element.47.refs_5_), channel_id=1, source_target_pairs={{0,31},{1,0},{2,1},{3,2},{4,3},{5,4},{6,5},{7,6},{8,7},{9,8},{10,9... | collective-permute-start | bytes 331784 | tf_op jit(solution)/shard_map/ppermute | solution.py:508
  50.1 3.5 %collective-permute-start.15 = (bf16[224,128]{1,0:T(8,128)(2,1)S(1)}, bf16[224,128]{1,0:T(8,128)(2,1)S(1)}, u32[]{:S(2)}, u32[]{:S(2)}) collective-permute-start(bf16[224,128]{1,0:T(8,128)(2,1)S(1)} %get-tuple-element.48), channel_id=1, source_target_pairs={{0,2},{1,3},{2,4},{3,5},{4,6},{5,7},{6,8},{7,9},{8,10},{9,11},{10,... | collective-permute-start | bytes 172040 | tf_op jit(solution)/shard_map/ppermute | solution.py:508
  53.6 0.0 collective-permute-start.16
  53.6 1.8 %collective-permute-done.15.refs_2_ = bf16[224,128]{1,0:T(8,128)(2,1)S(1)} collective-permute-done((bf16[224,128]{1,0:T(8,128)(2,1)S(1)}, bf16[224,128]{1,0:T(8,128)(2,1)S(1)}, u32[]{:S(2)}, u32[]{:S(2)}) %collective-permute-start.15) | collective-permute-done | bytes 57376 | tf_op jit(solution)/shard_map/ppermute | solution.py:508
  55.4 5.7 %collective-permute-done.16.refs_3_ = bf16[224,128]{1,0:T(8,128)(2,1)S(1)} collective-permute-done((bf16[224,128]{1,0:T(8,128)(2,1)S(1)}, bf16[224,128]{1,0:T(8,128)(2,1)S(1)}, u32[]{:S(2)}, u32[]{:S(2)}) %collective-permute-start.16) | collective-permute-done | bytes 57376 | tf_op jit(solution)/shard_map/ppermute | solution.py:508
  61.1 0.0 collective-permute-done.13.refs_0_
  61.1 0.0 collective-permute-done.14.refs_1_
  61.1 0.7 %copy-done.5 = s32[1,9]{1,0:T(1,128)S(1)} copy-done((s32[1,9]{1,0:T(1,128)S(1)}, s32[1,9]{1,0:T(1,128)}, u32[]{:S(2)}) %copy-start.5) | copy-done | bytes 60
  61.7 1.6 %second_join.1 = (bf16[1944,128]{1,0:T(8,128)(2,1)}, f32[9,128]{1,0:T(8,128)S(1)}) custom-call(f32[1]{0:T(128)S(6)} %copy.16.width_ref, f32[8]{0:T(128)S(1)} %copy-done.4, s32[1,9]{1,0:T(1,128)S(1)} %copy-done.5, bf16[432,128]{1,0:T(8,128)(2,1)S(1)} %collective-permute-done.13.refs_0_, bf16[432,128]{1,0:T(8,128)(2,1)S(1)} %collective-permute-done.14.refs_1_, ...), custom_call_target="tpu_custom_call" | custom-call | flops 10000000 | bytes 3000000 | tf_op jit(solution)/shard_map/second_join/pallas_call | solution.py:580
  63.3 0.6 copy.15
  (2 shorter events, 0.0 us)
Async XLA Ops:
  0.6 1.0 %copy-start = (bf16[3,1,8,9,9,128]{5,2,4,3,1,0:T(8,128)(2,1)S(1)}, bf16[3,1,8,9,9,128]{5,2,4,3,1,0:T(8,128)(2,1)}, u32[]{:S(2)}) copy-start(bf16[3,1,8,9,9,128]{5,2,4,3,1,0:T(8,128)(2,1)} %param.13) | copy-start | bytes 1492996
  1.7 6.6 %copy-start.1 = (bf16[3,1,8,9,9,128]{5,2,4,3,1,0:T(8,128)(2,1)S(1)}, bf16[3,1,8,9,9,128]{5,2,4,3,1,0:T(8,128)(2,1)}, u32[]{:S(2)}) copy-start(bf16[3,1,8,9,9,128]{5,2,4,3,1,0:T(8,128)(2,1)} %param.13) | copy-start | bytes 1492996
  1.9 5.6 %collective-permute-start.7 = (bf16[528,128]{1,0:T(8,128)(2,1)S(1)}, bf16[528,128]{1,0:T(8,128)(2,1)S(1)}, u32[]{:S(2)}, u32[]{:S(2)}) collective-permute-start(bf16[528,128]{1,0:T(8,128)(2,1)S(1)} %get-tuple-element.39), channel_id=1, source_target_pairs={{0,32},{32,0},{64,96},{96,64},{1,33},{33,1},{65,97},{97,65},{2,34}... | collective-permute-start | bytes 405512 | tf_op jit(solution)/shard_map/ppermute | solution.py:512
  2.0 8.0 %collective-permute-start.8 = (bf16[528,128]{1,0:T(8,128)(2,1)S(1)}, bf16[528,128]{1,0:T(8,128)(2,1)S(1)}, u32[]{:S(2)}, u32[]{:S(2)}) collective-permute-start(bf16[528,128]{1,0:T(8,128)(2,1)S(1)} %get-tuple-element.40), channel_id=1, source_target_pairs={{0,64},{32,96},{64,0},{96,32},{1,65},{33,97},{65,1},{97,33},{2,66}... | collective-permute-start | bytes 405512 | tf_op jit(solution)/shard_map/ppermute | solution.py:512
  4.0 6.8 %collective-permute-start.9 = (bf16[528,128]{1,0:T(8,128)(2,1)S(1)}, bf16[528,128]{1,0:T(8,128)(2,1)S(1)}, u32[]{:S(2)}, u32[]{:S(2)}) collective-permute-start(bf16[528,128]{1,0:T(8,128)(2,1)S(1)} %get-tuple-element.41), channel_id=1, source_target_pairs={{0,96},{32,64},{64,32},{96,0},{1,97},{33,65},{65,33},{97,1},{2,98}... | collective-permute-start | bytes 405512 | tf_op jit(solution)/shard_map/ppermute | solution.py:512
  4.1 1.0 %copy-start.2 = (bf16[3,1,8,9,9,128]{5,2,4,3,1,0:T(8,128)(2,1)S(1)}, bf16[3,1,8,9,9,128]{5,2,4,3,1,0:T(8,128)(2,1)}, u32[]{:S(2)}) copy-start(bf16[3,1,8,9,9,128]{5,2,4,3,1,0:T(8,128)(2,1)} %param.12) | copy-start | bytes 1492996
  5.1 3.1 %copy-start.3 = (f32[4,8,128]{2,1,0:T(8,128)S(1)}, f32[4,8,128]{2,1,0:T(8,128)}, u32[]{:S(2)}) copy-start(f32[4,8,128]{2,1,0:T(8,128)} %constant.20.clone.kappa_ref) | copy-start | bytes 49156
  5.1 11.5 %copy-start.11 = (bf16[352,528]{1,0:T(8,128)(2,1)S(1)}, bf16[352,528]{1,0:T(8,128)(2,1)}, u32[]{:S(2)}) copy-start(bf16[352,528]{1,0:T(8,128)(2,1)} %constant.24.clone.refs_11_) | copy-start | bytes 1115140
  5.3 6.8 %collective-permute-start.4 = (bf16[528,128]{1,0:T(8,128)(2,1)S(1)}, bf16[528,128]{1,0:T(8,128)(2,1)S(1)}, u32[]{:S(2)}, u32[]{:S(2)}) collective-permute-start(bf16[528,128]{1,0:T(8,128)(2,1)S(1)} %get-tuple-element.35), channel_id=1, source_target_pairs={{0,32},{32,0},{64,96},{96,64},{1,33},{33,1},{65,97},{97,65},{2,34}... | collective-permute-start | bytes 405512 | tf_op jit(solution)/shard_map/ppermute | solution.py:512
  5.6 8.7 %collective-permute-start.5 = (bf16[528,128]{1,0:T(8,128)(2,1)S(1)}, bf16[528,128]{1,0:T(8,128)(2,1)S(1)}, u32[]{:S(2)}, u32[]{:S(2)}) collective-permute-start(bf16[528,128]{1,0:T(8,128)(2,1)S(1)} %get-tuple-element.36), channel_id=1, source_target_pairs={{0,64},{32,96},{64,0},{96,32},{1,65},{33,97},{65,1},{97,33},{2,66}... | collective-permute-start | bytes 405512 | tf_op jit(solution)/shard_map/ppermute | solution.py:512
  7.5 0.7 %copy-start.4 = (f32[8]{0:T(128)S(1)}, f32[8]{0:T(128)}, u32[]{:S(2)}) copy-start(f32[8]{0:T(128)} %height_ref.7) | copy-start | bytes 100
  7.5 9.1 %copy-start.6 = (bf16[512,512]{1,0:T(8,128)(2,1)S(1)}, bf16[512,512]{1,0:T(8,128)(2,1)}, u32[]{:S(2)}) copy-start(bf16[512,512]{1,0:T(8,128)(2,1)} %constant.21.clone.refs_8_) | copy-start | bytes 1572868
  7.5 9.1 %collective-permute-start.6 = (bf16[528,128]{1,0:T(8,128)(2,1)S(1)}, bf16[528,128]{1,0:T(8,128)(2,1)S(1)}, u32[]{:S(2)}, u32[]{:S(2)}) collective-permute-start(bf16[528,128]{1,0:T(8,128)(2,1)S(1)} %get-tuple-element.37), channel_id=1, source_target_pairs={{0,96},{32,64},{64,32},{96,0},{1,97},{33,65},{65,33},{97,1},{2,98}... | collective-permute-start | bytes 405512 | tf_op jit(solution)/shard_map/ppermute | solution.py:512
  10.0 18.3 %collective-permute-start.2 = (bf16[224,128]{1,0:T(8,128)(2,1)S(1)}, bf16[224,128]{1,0:T(8,128)(2,1)S(1)}, u32[]{:S(2)}, u32[]{:S(2)}) collective-permute-start(bf16[224,128]{1,0:T(8,128)(2,1)S(1)} %get-tuple-element.30), channel_id=1, source_target_pairs={{0,2},{1,3},{2,4},{3,5},{4,6},{5,7},{6,8},{7,9},{8,10},{9,11},{10,... | collective-permute-start | bytes 172040 | tf_op jit(solution)/shard_map/ppermute | solution.py:508
  10.8 21.1 %collective-permute-start.3 = (bf16[224,128]{1,0:T(8,128)(2,1)S(1)}, bf16[224,128]{1,0:T(8,128)(2,1)S(1)}, u32[]{:S(2)}, u32[]{:S(2)}) collective-permute-start(bf16[224,128]{1,0:T(8,128)(2,1)S(1)} %get-tuple-element.31), channel_id=1, source_target_pairs={{0,30},{1,31},{2,0},{3,1},{4,2},{5,3},{6,4},{7,5},{8,6},{9,7},{10,... | collective-permute-start | bytes 172040 | tf_op jit(solution)/shard_map/ppermute | solution.py:508
  16.6 1.0 %copy-start.7 = (bf16[512,512]{1,0:T(8,128)(2,1)S(1)}, bf16[512,512]{1,0:T(8,128)(2,1)}, u32[]{:S(2)}) copy-start(bf16[512,512]{1,0:T(8,128)(2,1)} %constant.22.clone.refs_9_) | copy-start | bytes 1572868
  17.6 1.0 %copy-start.8 = (bf16[512,512]{1,0:T(8,128)(2,1)S(1)}, bf16[512,512]{1,0:T(8,128)(2,1)}, u32[]{:S(2)}) copy-start(bf16[512,512]{1,0:T(8,128)(2,1)} %constant.23.clone.refs_10_) | copy-start | bytes 1572868
  18.6 1.0 %copy-start.9 = (bf16[4,512,128]{2,1,0:T(8,128)(2,1)S(1)}, bf16[4,512,128]{2,1,0:T(8,128)(2,1)}, u32[]{:S(2)}) copy-start(bf16[4,512,128]{2,1,0:T(8,128)(2,1)} %constant.25.clone.refs_12_) | copy-start | bytes 1572868
  19.7 1.0 %copy-start.10 = (bf16[4,512,128]{2,1,0:T(8,128)(2,1)S(1)}, bf16[4,512,128]{2,1,0:T(8,128)(2,1)}, u32[]{:S(2)}) copy-start(bf16[4,512,128]{2,1,0:T(8,128)(2,1)} %constant.26.clone.refs_13_) | copy-start | bytes 1572868
  26.0 17.4 %collective-permute-start.10 = (bf16[528,128]{1,0:T(8,128)(2,1)S(1)}, bf16[528,128]{1,0:T(8,128)(2,1)S(1)}, u32[]{:S(2)}, u32[]{:S(2)}) collective-permute-start(bf16[528,128]{1,0:T(8,128)(2,1)S(1)} %get-tuple-element.43), channel_id=1, source_target_pairs={{0,32},{32,0},{64,96},{96,64},{1,33},{33,1},{65,97},{97,65},{2,34}... | collective-permute-start | bytes 405512 | tf_op jit(solution)/shard_map/ppermute | solution.py:512
  26.5 17.0 %collective-permute-start.11 = (bf16[528,128]{1,0:T(8,128)(2,1)S(1)}, bf16[528,128]{1,0:T(8,128)(2,1)S(1)}, u32[]{:S(2)}, u32[]{:S(2)}) collective-permute-start(bf16[528,128]{1,0:T(8,128)(2,1)S(1)} %get-tuple-element.44), channel_id=1, source_target_pairs={{0,64},{32,96},{64,0},{96,32},{1,65},{33,97},{65,1},{97,33},{2,66}... | collective-permute-start | bytes 405512 | tf_op jit(solution)/shard_map/ppermute | solution.py:512
  28.3 15.2 %collective-permute-start.12 = (bf16[528,128]{1,0:T(8,128)(2,1)S(1)}, bf16[528,128]{1,0:T(8,128)(2,1)S(1)}, u32[]{:S(2)}, u32[]{:S(2)}) collective-permute-start(bf16[528,128]{1,0:T(8,128)(2,1)S(1)} %get-tuple-element.45), channel_id=1, source_target_pairs={{0,96},{32,64},{64,32},{96,0},{1,97},{33,65},{65,33},{97,1},{2,98}... | collective-permute-start | bytes 405512 | tf_op jit(solution)/shard_map/ppermute | solution.py:512
  28.3 8.4 %collective-permute-start = (bf16[448,128]{1,0:T(8,128)(2,1)S(1)}, bf16[448,128]{1,0:T(8,128)(2,1)S(1)}, u32[]{:S(2)}, u32[]{:S(2)}) collective-permute-start(bf16[448,128]{1,0:T(8,128)(2,1)S(1)} %get-tuple-element.28.refs_4_), channel_id=1, source_target_pairs={{0,1},{1,2},{2,3},{3,4},{4,5},{5,6},{6,7},{7,8},{8,9},{9,10},{10,1... | collective-permute-start | bytes 344072 | tf_op jit(solution)/shard_map/ppermute | solution.py:508
  31.9 11.4 %collective-permute-start.1 = (bf16[448,128]{1,0:T(8,128)(2,1)S(1)}, bf16[448,128]{1,0:T(8,128)(2,1)S(1)}, u32[]{:S(2)}, u32[]{:S(2)}) collective-permute-start(bf16[448,128]{1,0:T(8,128)(2,1)S(1)} %get-tuple-element.29.refs_5_), channel_id=1, source_target_pairs={{0,31},{1,0},{2,1},{3,2},{4,3},{5,4},{6,5},{7,6},{8,7},{9,8},{10,9... | collective-permute-start | bytes 344072 | tf_op jit(solution)/shard_map/ppermute | solution.py:508
  45.6 15.5 %collective-permute-start.13 = (bf16[432,128]{1,0:T(8,128)(2,1)S(1)}, bf16[432,128]{1,0:T(8,128)(2,1)S(1)}, u32[]{:S(2)}, u32[]{:S(2)}) collective-permute-start(bf16[432,128]{1,0:T(8,128)(2,1)S(1)} %get-tuple-element.46.refs_4_), channel_id=1, source_target_pairs={{0,1},{1,2},{2,3},{3,4},{4,5},{5,6},{6,7},{7,8},{8,9},{9,10},{10,1... | collective-permute-start | bytes 331784 | tf_op jit(solution)/shard_map/ppermute | solution.py:508
  45.7 15.4 %collective-permute-start.14 = (bf16[432,128]{1,0:T(8,128)(2,1)S(1)}, bf16[432,128]{1,0:T(8,128)(2,1)S(1)}, u32[]{:S(2)}, u32[]{:S(2)}) collective-permute-start(bf16[432,128]{1,0:T(8,128)(2,1)S(1)} %get-tuple-element.47.refs_5_), channel_id=1, source_target_pairs={{0,31},{1,0},{2,1},{3,2},{4,3},{5,4},{6,5},{7,6},{8,7},{9,8},{10,9... | collective-permute-start | bytes 331784 | tf_op jit(solution)/shard_map/ppermute | solution.py:508
  50.1 5.3 %collective-permute-start.15 = (bf16[224,128]{1,0:T(8,128)(2,1)S(1)}, bf16[224,128]{1,0:T(8,128)(2,1)S(1)}, u32[]{:S(2)}, u32[]{:S(2)}) collective-permute-start(bf16[224,128]{1,0:T(8,128)(2,1)S(1)} %get-tuple-element.48), channel_id=1, source_target_pairs={{0,2},{1,3},{2,4},{3,5},{4,6},{5,7},{6,8},{7,9},{8,10},{9,11},{10,... | collective-permute-start | bytes 172040 | tf_op jit(solution)/shard_map/ppermute | solution.py:508
  53.6 7.5 %collective-permute-start.16 = (bf16[224,128]{1,0:T(8,128)(2,1)S(1)}, bf16[224,128]{1,0:T(8,128)(2,1)S(1)}, u32[]{:S(2)}, u32[]{:S(2)}) collective-permute-start(bf16[224,128]{1,0:T(8,128)(2,1)S(1)} %get-tuple-element.49), channel_id=1, source_target_pairs={{0,30},{1,31},{2,0},{3,1},{4,2},{5,3},{6,4},{7,5},{8,6},{9,7},{10,... | collective-permute-start | bytes 172040 | tf_op jit(solution)/shard_map/ppermute | solution.py:508
  61.1 0.7 %copy-start.5 = (s32[1,9]{1,0:T(1,128)S(1)}, s32[1,9]{1,0:T(1,128)}, u32[]{:S(2)}) copy-start(s32[1,9]{1,0:T(1,128)} %mask_ref.1) | copy-start | bytes 112
where the time goes:
time: 64.3 us; the launch traced here: 63.9 us
  waiting for transfers between devices  23 us (36%)
  starting transfers between devices  20.5 us (32%)
  Pallas kernels  11.5 us (18%)
  local copies, waits for them, and re-layouts  7.49 us (12%)
  between operations  1.48 us (2%)
    ppermute x8, waiting for transfers between devices, ring(): lax.ppermute(value, 'xsec', [(n, (n + shift) % count) for n in range(coun...  18 us
    ppermute x8, starting transfers between devices, ring(): lax.ppermute(value, 'xsec', [(n, (n + shift) % count) for n in range(coun...  13.9 us
    unnamed x25, local copies, waits for them, and re-layouts  7.49 us
    ppermute x9, starting transfers between devices, swap(): lax.ppermute(value, 'span', [(n, n ^ flip) for n in range(lax.axis_size('...  6.55 us
    pallas_call x1, Pallas kernels, forcing(): call(force_kernel, 'adjoint_forcing', [((ROWS, 128), BF16)] * 4, [pltpu.V...  5.29 us
    ppermute x9, waiting for transfers between devices, swap(): lax.ppermute(value, 'span', [(n, n ^ flip) for n in range(lax.axis_size('...  5.03 us
    pallas_call x1, Pallas kernels, local(): call(second_kernel, 'second_substep', state_shapes + [((16 * COLS, 128),...  2.13 us
    pallas_call x1, Pallas kernels, local(): call(first_kernel, 'first_substep', state_shapes + [((16 * COLS + 16, 128...  1.75 us
  transfers between devices with their start and end apart: 17, of which 7 were waited for; matrix products, arithmetic and copies ran while one was open for 0% of the time, Pallas kernels for 12%

commit v1 on v0

--- a/solution.py
+++ b/solution.py
@@ -76,8 +76,7 @@
         both[1, layer, :PLANE, layer, :PLANE] = around
     high, low = halves(both.reshape(4 * PAD, 2 * PAD))
     slope = np.concatenate([high, low, high], axis=1)
-    kappa = np.broadcast_to(kappa_sq.reshape(4, 1, 128), (4, 8, 128)).astype(np.float32)
-    return synthesis.astype(jnp.bfloat16), halves(wave), slope, halves(analysis), kappa
+    return synthesis.astype(jnp.bfloat16), halves(wave), slope, halves(analysis)
 
 
 def smem():
@@ -88,79 +87,135 @@
     return pl.BlockSpec(memory_space=pltpu.VMEM)
 
 
-def call(kernel, name, outs, scratch, specs, flops, nbytes):
+def hbm():
+    return pl.BlockSpec(memory_space=pltpu.HBM)
+
+
+def in_hbm(value):
+    return pltpu.with_memory_space_constraint(value, pltpu.HBM)
+
+
+def call(kernel, name, outs, scratch, specs, flops, nbytes, mib):
     return pl.pallas_call(
         kernel,
         out_shape=[jax.ShapeDtypeStruct(shape, kind) for shape, kind in outs],
         in_specs=specs,
         out_specs=[vmem() for _ in outs],
         scratch_shapes=scratch,
-        compiler_params=pltpu.CompilerParams(vmem_limit_bytes=40 * MIB),
+        compiler_params=pltpu.CompilerParams(vmem_limit_bytes=mib * MIB),
         cost_estimate=pl.CostEstimate(flops=flops, bytes_accessed=nbytes, transcendentals=0),
         name=name,
     )
 
 
-def repack_kernel(pos_ref, x_ref, *refs):
-    outs, wide = refs[:4], refs[4]
+def repack_kernel(pos_ref, width_ref, adj_hbm, fwd_hbm, height_hbm, mask_hbm, *refs):
+    groups, wide_adj, shape_ref = refs[0:4], refs[4], refs[5]
+    adj_ref, fwd_ref, wide_fwd, height_ref, mask_ref, sems = refs[6:12]
+    pairs = (
+        (adj_hbm, adj_ref),
+        (fwd_hbm, fwd_ref),
+        (height_hbm, height_ref),
+        (mask_hbm, mask_ref),
+    )
+    copies = [
+        pltpu.make_async_copy(source, target, sems.at[n])
+        for n, (source, target) in enumerate(pairs)
+    ]
+    for copy in copies:
+        copy.start()
     pos = pos_ref[0]
-    wide[pl.ds(0, POINTS), :] = x_ref[...].astype(F32)
     keep = lax.broadcasted_iota(jnp.int32, (PAD, 128), 0) < PLANE
-    for flip, out in enumerate(outs):
-        group = pos ^ flip
-        for comp in range(3):
-            parts = []
-            for layer in range(2):
-                start = comp * PLANE * 8 + 2 * group + layer
-                rows = wide[pl.ds(start, PAD, stride=8), :]
-                parts.append(jnp.where(keep, rows, 0.0))
-            block = jnp.concatenate(parts, axis=0).astype(BF16)
-            out[comp * 2 * PAD : (comp + 1) * 2 * PAD, :] = block
-
-
-def repack(pos, field, name):
+    for which, (x_ref, wide) in enumerate(((adj_ref, wide_adj), (fwd_ref, wide_fwd))):
+        copies[which].wait()
+        wide[pl.ds(0, POINTS), :] = x_ref[...].astype(F32)
+        for flip, out in enumerate(groups):
+            group = pos ^ flip
+            for comp in range(3):
+                parts = []
+                for layer in range(2):
+                    start = comp * PLANE * 8 + 2 * group + layer
+                    rows = wide[pl.ds(start, PAD, stride=8), :]
+                    parts.append(jnp.where(keep, rows, 0.0))
+                block = jnp.concatenate(parts, axis=0).astype(BF16)
+                at = which * ROWS + comp * 2 * PAD
+                out[at : at + 2 * PAD, :] = block
+    for copy in copies[2:]:
+        copy.wait()
+
+    def spread(value):
+        return jnp.full((8, 128), value, F32)
+
+    layer = lax.broadcasted_iota(jnp.int32, (8, 128), 0)
+    height = spread(height_ref[0])
+    for index in range(1, 8):
+        height = jnp.where(layer == index, height_ref[index], height)
+    shape_ref[0:8, :] = 2.0 / height
+    shape_ref[8:16, :] = 2.0 / spread(width_ref[0])
+    shape_ref[16:24, :] = 2.0 / spread(height_ref[2 * pos])
+    shape_ref[24:32, :] = 2.0 / spread(height_ref[2 * pos + 1])
+    wall = WALL_GAIN * (2.0 / spread(height_ref[0]))
+    for j in range(NODES):
+        shape_ref[32 + 8 * j : 40 + 8 * j, :] = wall * mask_ref[0, j].astype(F32)
+
+
+def repack(pos, adj, fwd, heights, widths, mask):
     return call(
         repack_kernel,
-        name,
-        [((ROWS, 128), BF16)] * 4,
-        [pltpu.VMEM((POINTS + 56, 128), F32)],
-        [smem(), vmem()],
+        "span_groups",
+        [((2 * ROWS, 128), BF16)] * 4
+        + [((POINTS + 56, 128), F32), ((32 + 8 * NODES, 128), F32)],
+        [
+            pltpu.VMEM((POINTS, 128), BF16),
+            pltpu.VMEM((POINTS, 128), BF16),
+            pltpu.VMEM((POINTS + 56, 128), F32),
+            pltpu.SMEM((8,), F32),
+            pltpu.SMEM((1, NODES), jnp.int32),
+            pltpu.SemaphoreType.DMA((4,)),
+        ],
+        [smem()] * 2 + [hbm()] * 4,
         1_000_000,
-        1_000_000,
-    )(pos, field)
-
-
-def force_kernel(
-    pos_ref, height_ref, width_ref, *refs
-):
-    fwd, adj = refs[0:4], refs[4:8]
-    synth_ref, wave_hi_ref, wave_lo_ref, slope_ref, an_hi_ref, an_lo_ref = refs[8:14]
-    outs = refs[14:18]
-    planes, zplanes, grads, force = refs[18:22]
+        2_000_000,
+        12,
+    )(pos, widths, *map(in_hbm, (adj, fwd, heights, mask)))
+
+
+def gather(ref, pos):
+    parts = [ref[pl.ds(pl.multiple_of(128 * (pos ^ flip), 128), 128), :] for flip in range(4)]
+    return jnp.concatenate(parts, axis=0)
+
+
+def transform(pos, which, chunks, tables, planes, zplanes, grads):
+    synth_ref, wave_hi_ref, wave_lo_ref, slope_ref = tables
+    rows = slice(which * ROWS, (which + 1) * ROWS)
+    modes = jnp.concatenate([chunk[rows, :] for chunk in chunks], axis=1)
+    planes[...] = jnp.dot(modes, gather(synth_ref, pos), preferred_element_type=F32)
+    zplanes[...] = jnp.dot(
+        modes, gather(wave_hi_ref, pos), preferred_element_type=F32
+    ) + jnp.dot(modes, gather(wave_lo_ref, pos), preferred_element_type=F32)
+    slope = slope_ref[...]
+    for comp in range(3):
+        block = planes[comp * 2 * PAD : (comp + 1) * 2 * PAD, :]
+        high = block.astype(BF16)
+        low = (block - high.astype(F32)).astype(BF16)
+        stack = jnp.concatenate([high, high, low], axis=0)
+        grads[comp] = jnp.dot(slope, stack, preferred_element_type=F32)
+
+
+def force_kernel(pos_ref, shape_ref, *refs):
+    chunks, tables = refs[0:4], refs[4:10]
+    outs = refs[10:14]
+    adj_planes, adj_zplanes, adj_grads = refs[14:17]
+    fwd_planes, fwd_zplanes, fwd_grads, force = refs[17:21]
+    an_hi_ref, an_lo_ref = tables[4:]
     pos = pos_ref[0]
-
-    def gather(ref):
-        parts = [ref[pl.ds(pl.multiple_of(128 * (pos ^ flip), 128), 128), :] for flip in range(4)]
-        return jnp.concatenate(parts, axis=0)
-
-    synth, wave_hi, wave_lo = gather(synth_ref), gather(wave_hi_ref), gather(wave_lo_ref)
-    slope = slope_ref[...]
-    for which, chunks in ((0, fwd), (1, adj)):
-        modes = jnp.concatenate([chunk[...] for chunk in chunks], axis=1)
-        planes[which] = jnp.dot(modes, synth, preferred_element_type=F32)
-        zplanes[which] = jnp.dot(modes, wave_hi, preferred_element_type=F32) + jnp.dot(
-            modes, wave_lo, preferred_element_type=F32
-        )
-        for comp in range(3):
-            block = planes[which, comp * 2 * PAD : (comp + 1) * 2 * PAD, :]
-            high = block.astype(BF16)
-            low = (block - high.astype(F32)).astype(BF16)
-            stack = jnp.concatenate([high, high, low], axis=0)
-            grads[which, comp] = jnp.dot(slope, stack, preferred_element_type=F32)
-
-    across = 2.0 / jnp.full((8, 128), width_ref[0], F32)
+    transform(pos, 0, chunks, tables[:4], adj_planes, adj_zplanes, adj_grads)
+    transform(pos, 1, chunks, tables[:4], fwd_planes, fwd_zplanes, fwd_grads)
+    planes, zplanes = (fwd_planes, adj_planes), (fwd_zplanes, adj_zplanes)
+    grads = (fwd_grads, adj_grads)
+
+    across = shape_ref[8:16, :]
     for layer in range(2):
-        along = 2.0 / jnp.full((8, 128), height_ref[2 * pos + layer], F32)
+        along = shape_ref[16 + 8 * layer : 24 + 8 * layer, :]
         for tile in range(PAD // 8):
             row = layer * PAD + 8 * tile
             for lane in range(0, NK, 128):
@@ -168,15 +223,15 @@
 
                 def plane(which, comp):
                     at = comp * 2 * PAD + row
-                    return planes[which, at : at + 8, lanes]
+                    return planes[which][at : at + 8, lanes]
 
                 def zplane(which, comp):
                     at = comp * 2 * PAD + row
-                    return zplanes[which, at : at + 8, lanes]
+                    return zplanes[which][at : at + 8, lanes]
 
                 def grad(which, direc, comp):
                     at = direc * 2 * PAD + row
-                    return grads[which, comp, at : at + 8, lanes]
+                    return grads[which][comp, at : at + 8, lanes]
 
                 fwd_r = plane(0, 0) * along
                 fwd_t = plane(0, 1) * across
@@ -210,31 +265,22 @@
         out[...] = result[:, 128 * flip : 128 * (flip + 1)]
 
 
-def forcing(pos, heights, widths, fwd, adj, tables):
-    synth, (wave_hi, wave_lo), slope, (an_hi, an_lo) = tables
-    split = lambda table: jnp.asarray(table.reshape(NK, 4, 128).transpose(1, 0, 2))
-    constants = [
-        jnp.asarray(synth),
-        jnp.asarray(wave_hi),
-        jnp.asarray(wave_lo),
-        jnp.asarray(slope),
-        split(an_hi),
-        split(an_lo),
-    ]
+def plane_shapes():
+    return [(ROWS, NK), (ROWS, NK), (3, 4 * PAD, NK)]
+
+
+def forcing(pos, shape, chunks, tables):
+    fields = [pltpu.VMEM(shape, F32) for shape in plane_shapes()]
     return call(
         force_kernel,
         "adjoint_forcing",
         [((ROWS, 128), BF16)] * 4,
-        [
-            pltpu.VMEM((2, ROWS, NK), F32),
-            pltpu.VMEM((2, ROWS, NK), F32),
-            pltpu.VMEM((2, 3, 4 * PAD, NK), F32),
-            pltpu.VMEM((ROWS, NK), F32),
-        ],
-        [smem(), smem(), smem()] + [vmem()] * 14,
+        fields + fields + [pltpu.VMEM((ROWS, NK), F32)],
+        [smem()] + [vmem()] * 11,
         5_000_000_000,
         8_000_000,
-    )(pos, heights, widths, *fwd, *adj, *constants)
+        20,
+    )(pos, shape, *chunks, *tables)
 
 
 def mirror(matrix):
@@ -272,12 +318,15 @@
     return low + [even[4]] + high[::-1]
 
 
-def layer_vectors(height_ref):
+def wave_squares(pos):
+    index = lax.broadcasted_iota(jnp.int32, (8, 128), 1) + 128 * pos
+    wave = jnp.where(index == 1, NK // 2, index >> 1).astype(F32) * SPAN_GAIN
+    return wave * wave
+
+
+def layer_vectors(shape_ref):
     layer = lax.broadcasted_iota(jnp.int32, (8, 128), 0)
-    height = jnp.full((8, 128), height_ref[0], F32)
-    for index in range(1, 8):
-        height = jnp.where(layer == index, height_ref[index], height)
-    along = 2.0 / height
+    along = shape_ref[0:8, :]
     below = pltpu.roll(along, 1, 0)
     above = pltpu.roll(along, 7, 0)
     bottom, top = layer == 0, layer == 7
@@ -288,6 +337,7 @@
     return dict(
         layer=layer,
         along=along,
+        across=shape_ref[8:16, :],
         own_low=own_low,
         own_high=own_high,
         from_below=from_below,
@@ -297,8 +347,8 @@
     )
 
 
-def local_step(vec, width, kappa, load, store, sent, two_away, visc, faces):
-    across = 2.0 / jnp.full((8, 128), width, F32)
+def local_step(vec, kappa, load, store, sent, two_away, visc, faces):
+    across = vec["across"]
     scale_t = DIFFUSE * across * across
     scale_r = DIFFUSE * vec["along"] * vec["along"]
     scale_k = DIFFUSE * kappa
@@ -364,16 +414,22 @@
             else:
                 second = jnp.zeros((8, 128), F32)
             ref[pl.ds(16 * block, 16), :] = jnp.concatenate([first, second], axis=0).astype(BF16)
-    return across
 
 
 def spot(comp, i, j):
     return pl.ds(8 * ((comp * NODES + i) * NODES + j), 8)
 
 
-def first_kernel(pos_ref, height_ref, width_ref, kappa_ref, x_ref, *refs):
-    out, right, left, right_far, left_far, wide, visc, faces = refs
-    wide[...] = x_ref[...].astype(F32)
+def first_kernel(pos_ref, shape_ref, wide, *refs):
+    given, refs = refs[0:6], refs[6:]
+    out, right, left, right_far, left_far = refs[0:5]
+    tables, (visc, faces, sems) = refs[5:11], refs[11:14]
+    copies = [
+        pltpu.make_async_copy(source, target, sems.at[n])
+        for n, (source, target) in enumerate(zip(given, tables))
+    ]
+    for copy in copies:
+        copy.start()
 
     def load(comp, i, j):
         return wide[spot(comp, i, j), :]
@@ -381,11 +437,10 @@
     def store(comp, i, j, value, step):
         out[spot(comp, i, j), :] = value + step
 
-    vec = layer_vectors(height_ref)
-    kappa = kappa_ref[pos_ref[0]]
-    across = local_step(
-        vec, width_ref[0], kappa, load, store, (right, left), (right_far, left_far), visc, faces
-    )
+    vec = layer_vectors(shape_ref)
+    kappa = wave_squares(pos_ref[0])
+    local_step(vec, kappa, load, store, (right, left), (right_far, left_far), visc, faces)
+    across = vec["across"]
     high = across.astype(BF16).astype(F32)
     mid = (across - high).astype(BF16).astype(F32)
     low = across - high - mid
@@ -394,9 +449,11 @@
     block = jnp.concatenate([note, jnp.zeros((8, 128), F32)], axis=0).astype(BF16)
     for ref in (right, left):
         ref[pl.ds(16 * COLS, 16), :] = block
-
-
-def second_kernel(pos_ref, height_ref, width_ref, kappa_ref, base_ref, *refs):
+    for copy in copies:
+        copy.wait()
+
+
+def second_kernel(pos_ref, shape_ref, base_ref, *refs):
     chunks = refs[:4]
     out, right, left, right_far, left_far, push, wide, visc, faces = refs[4:]
     pos = pos_ref[0]
@@ -407,7 +464,7 @@
             for layer in range(2):
                 start = comp * PLANE * 8 + 2 * group + layer
                 push[pl.ds(start, PLANE, stride=8), :] = block[layer * PAD : layer * PAD + PLANE]
-    vec = layer_vectors(height_ref)
+    vec = layer_vectors(shape_ref)
     off_wall = jnp.where(vec["layer"] == 0, 0.0, 1.0)
     for comp in range(3):
         for i in range(NODES):
@@ -425,8 +482,7 @@
 
     local_step(
         vec,
-        width_ref[0],
-        kappa_ref[pos],
+        wave_squares(pos),
         load,
         store,
         (right, left),
@@ -436,11 +492,11 @@
     )
 
 
-def join_step(width, near, far, own, sides, state, store):
+def join_step(shape_ref, near, far, own, sides, state, store):
     from_left, from_right = near
     far_left, far_right = far
     own_right, own_left = own
-    across = 2.0 / jnp.full((8, 128), width, F32)
+    across = shape_ref[8:16, :]
     gain = (0.5 * DIFFUSE) * across
     gain_left, gain_right = (0.5 * DIFFUSE) * sides[0], (0.5 * DIFFUSE) * sides[1]
     for block in range(14):
@@ -468,7 +524,7 @@
                 store(comp, i, j, state[spot(comp, i, j), :] + add)
 
 
-def first_join_kernel(width_ref, *refs):
+def first_join_kernel(shape_ref, *refs):
     near, far, own = refs[0:2], refs[2:4], refs[4:6]
     state, out, sides_out = refs[6:9]
     sides = []
@@ -481,10 +537,10 @@
     def store(comp, i, j, value):
         out[spot(comp, i, j), :] = value
 
-    join_step(width_ref[0], near, far, own, sides, state, store)
-
-
-def second_join_kernel(width_ref, height_ref, mask_ref, *refs):
+    join_step(shape_ref, near, far, own, sides, state, store)
+
+
+def second_join_kernel(shape_ref, *refs):
     near, far, own = refs[0:2], refs[2:4], refs[4:6]
     sides_ref, state, out, wall, full = refs[6:11]
     sides = [sides_ref[pl.ds(0, 8), :], sides_ref[pl.ds(8, 8), :]]
@@ -494,13 +550,12 @@
     def store(comp, i, j, value):
         full[spot(comp, i, j), :] = value * off_wall if i == 0 else value
 
-    join_step(width_ref[0], near, far, own, sides, state, store)
+    join_step(shape_ref, near, far, own, sides, state, store)
     out[...] = full[...].astype(BF16)
-    along = 2.0 / jnp.full((8, 128), height_ref[0], F32)
     for j in range(NODES):
         rows = weighted(DERIV[0], [full[spot(0, i, j), :] for i in range(NODES)])
-        rows = (WALL_GAIN * along) * rows * mask_ref[0, j].astype(F32)
-        wall[pl.ds(j, 1), :] = rows[0:1]
+        rows = rows * shape_ref[pl.ds(32 + 8 * j, 8), :]
+        wall[j] = rows[0:1]
 
 
 def ring(value, shift):
@@ -512,82 +567,89 @@
     return lax.ppermute(value, "span", [(n, n ^ flip) for n in range(lax.axis_size("span"))])
 
 
-def halo(right, left, right_far, left_far):
-    from_left, from_right = ring(right, 1), ring(left, -1)
-    far_left, far_right = ring(right_far, 2), ring(left_far, -2)
-    return from_left, from_right, far_left, far_right
+def halo(right, left, shift):
+    return [ring(right, shift), ring(left, -shift)]
 
 
 def local(fwd_modes, adj_modes, layer_height, column_width, wall_mask):
-    synth, wave, slope, analysis, kappa = plane_tables()
-    kappa = jnp.asarray(kappa)
+    synth, (wave_hi, wave_lo), slope, (an_hi, an_lo) = plane_tables()
+    split = lambda table: table.reshape(NK, 4, 128).transpose(1, 0, 2)
+    constants = [
+        jnp.asarray(table)
+        for table in (synth, wave_hi, wave_lo, slope, split(an_hi), split(an_lo))
+    ]
     pos = lax.axis_index("span").astype(jnp.int32).reshape(1)
 
     def resident(field):
         return field.transpose(0, 1, 3, 4, 2, 5).reshape(POINTS, 128)
 
     fwd_flat, adj_flat = resident(fwd_modes), resident(adj_modes)
-    state_shapes = [((POINTS, 128), F32)]
+    state_shape = ((POINTS, 128), F32)
     far_shapes = [((224, 128), BF16)] * 2
-    work = [
-        pltpu.VMEM((POINTS, 128), F32),
-        pltpu.VMEM((PLANE * 8, 128), F32),
-        pltpu.VMEM((2 * COLS * 8, 128), F32),
-    ]
-
-    adj_own, *adj_away = repack(pos, adj_flat, "adj_groups")
-    adj_all = [adj_own] + [swap(part, flip + 1) for flip, part in enumerate(adj_away)]
-    fwd_own, *fwd_away = repack(pos, fwd_flat, "fwd_groups")
-    fwd_all = [fwd_own] + [swap(part, flip + 1) for flip, part in enumerate(fwd_away)]
-
-    state, right, left, right_far, left_far = call(
+    work = [pltpu.VMEM((PLANE * 8, 128), F32), pltpu.VMEM((2 * COLS * 8, 128), F32)]
+
+    def exchange(parts):
+        return [parts[0]] + [swap(part, flip + 1) for flip, part in enumerate(parts[1:])]
+
+    *groups, adj_wide, shape = repack(
+        pos, adj_flat, fwd_flat, layer_height, column_width, wall_mask
+    )
+    chunks = exchange(groups)
+
+    state, right, left, right_far, left_far, *tables = call(
         first_kernel,
         "first_substep",
-        state_shapes + [((16 * COLS + 16, 128), BF16)] * 2 + far_shapes,
-        work,
-        [smem(), smem(), smem(), vmem(), vmem()],
+        [state_shape]
+        + [((16 * COLS + 16, 128), BF16)] * 2
+        + far_shapes
+        + [(table.shape, BF16) for table in constants],
+        work + [pltpu.SemaphoreType.DMA((6,))],
+        [smem()] + [vmem()] * 2 + [hbm()] * 6,
         50_000_000,
         3_000_000,
-    )(pos, layer_height, column_width, kappa, adj_flat)
-    got = halo(right, left, right_far, left_far)
-
-    parts = forcing(
-        pos, layer_height, column_width, fwd_all, adj_all, (synth, wave, slope, analysis)
-    )
-    parts = [parts[0]] + [swap(part, flip + 1) for flip, part in enumerate(parts[1:])]
+        10,
+    )(pos, shape, adj_wide, *map(in_hbm, constants))
+    near, far = halo(right, left, 1), halo(right_far, left_far, 2)
+    *far, chunks[0] = lax.optimization_barrier((*far, chunks[0]))
+    parts = forcing(pos, shape, chunks, tables)
+    *near, parts = lax.optimization_barrier((*near, tuple(parts)))
+    parts = exchange(parts)
 
     base, sides = call(
         first_join_kernel,
         "first_join",
-        state_shapes + [((16, 128), F32)],
+        [state_shape, ((16, 128), F32)],
         [],
-        [smem()] + [vmem()] * 7,
+        [vmem()] * 8,
         10_000_000,
         3_000_000,
-    )(column_width, *got, right, left, state)
+        8,
+    )(shape, *near, *far, right, left, state)
 
     state, right, left, right_far, left_far = call(
         second_kernel,
         "second_substep",
-        state_shapes + [((16 * COLS, 128), BF16)] * 2 + far_shapes,
-        [pltpu.VMEM((POINTS, 128), F32)] + work,
-        [smem(), smem(), smem()] + [vmem()] * 6,
+        [state_shape] + [((16 * COLS, 128), BF16)] * 2 + far_shapes,
+        [pltpu.VMEM((POINTS, 128), F32)] * 2 + work,
+        [smem()] + [vmem()] * 6,
         50_000_000,
         4_000_000,
-    )(pos, layer_height, column_width, kappa, base, *parts)
-    got = halo(right, left, right_far, left_far)
+        12,
+    )(pos, shape, base, *parts)
+    got = halo(right, left, 1) + halo(right_far, left_far, 2)
 
     adj_new, wall = call(
         second_join_kernel,
         "second_join",
-        [((POINTS, 128), BF16), ((NODES, 128), F32)],
+        [((POINTS, 128), BF16), ((NODES, 1, 128), F32)],
         [pltpu.VMEM((POINTS, 128), F32)],
-        [smem()] * 3 + [vmem()] * 8,
+        [vmem()] * 9,
         10_000_000,
         3_000_000,
-    )(column_width, layer_height, wall_mask, *got, right, left, sides, state)
+        8,
+    )(shape, *got, right, left, sides, state)
     adj_new = adj_new.reshape(3, 1, NODES, NODES, 8, 128).transpose(0, 1, 4, 2, 3, 5)
-    return adj_new, wall.reshape(1, NODES, 128)
+    return adj_new, wall.transpose(1, 0, 2)
 
 
 def solution(mesh):

time: 64.3 us -> 54.6 us (0.85)
  local copies, waits for them, and re-layouts: 7.49 us -> 0 us
  waiting for transfers between devices: 23 us -> 21 us
    unnamed x25 -> x0, local copies, waits for them, and re-layouts: 7.49 us -> none
    ppermute x8, waiting for transfers between devices: 18 us -> 13.3 us  [ring(): lax.ppermute(value, 'xsec', [(n, (n + shift) % count) for n in range(coun...]
    ppermute x8, starting transfers between devices: 13.9 us -> 17 us  [ring(): lax.ppermute(value, 'xsec', [(n, (n + shift) % count) for n in range(coun...]
    ppermute x9 -> x6, waiting for transfers between devices: 5.03 us -> 7.68 us  [swap(): lax.ppermute(value, 'span', [(n, n ^ flip) for n in range(lax.axis_size('...]
    ppermute x9 -> x6, starting transfers between devices: 6.55 us -> 4 us  [swap(): lax.ppermute(value, 'span', [(n, n ^ flip) for n in range(lax.axis_size('...]
    pallas_call x6 -> x5, Pallas kernels: 9.87 us -> 10 us  [the longest x1 4.82 us: forcing(): call(force_kernel, 'adjoint_forcing', [((ROWS, 128), BF16)] * 4, fields +...]
  transfers between devices with their start and end apart: 17 -> 14, of which waited for: 7 -> 7; matrix products, arithmetic and copies ran while one was open for 0% -> 0% of each run, Pallas kernels for 12% -> 13%
where the time goes in v1:
time: 54.6 us; the launch traced here: 54.4 us
  starting transfers between devices  21 us (38%)
  waiting for transfers between devices  21 us (38%)
  Pallas kernels  11.1 us (20%)
  between operations  1.35 us (2%)
    ppermute x8, starting transfers between devices, ring(): lax.ppermute(value, 'xsec', [(n, (n + shift) % count) for n in range(coun...  17 us
    ppermute x8, waiting for transfers between devices, ring(): lax.ppermute(value, 'xsec', [(n, (n + shift) % count) for n in range(coun...  13.3 us
    ppermute x6, waiting for transfers between devices, swap(): lax.ppermute(value, 'span', [(n, n ^ flip) for n in range(lax.axis_size('...  7.68 us
    pallas_call x1, Pallas kernels, forcing(): call(force_kernel, 'adjoint_forcing', [((ROWS, 128), BF16)] * 4, fields +...  4.82 us
    ppermute x6, starting transfers between devices, swap(): lax.ppermute(value, 'span', [(n, n ^ flip) for n in range(lax.axis_size('...  4 us
    pallas_call x1, Pallas kernels, local(): call(first_kernel, 'first_substep', [state_shape] + [((16 * COLS + 16, 12...  1.87 us
    pallas_call x1, Pallas kernels, repack(): call(repack_kernel, 'span_groups', [((2 * ROWS, 128), BF16)] * 4 + [((POI...  1.58 us
    pallas_call x1, Pallas kernels, local(): call(second_kernel, 'second_substep', [state_shape] + [((16 * COLS, 128),...  1.56 us
  transfers between devices with their start and end apart: 14, of which 7 were waited for; matrix products, arithmetic and copies ran while one was open for 0% of the time, Pallas kernels for 13%

profile of v1, /device:TPU:30, one launch (start us, length us, event | category | flops | bytes accessed | tf_op | source)
XLA Modules:
  0.0 54.4 jit_solution(11309262798644863704)
XLA Ops:
  1.3 1.6 %span_groups.1 = (bf16[1056,128]{1,0:T(8,128)(2,1)S(1)}, bf16[1056,128]{1,0:T(8,128)(2,1)S(1)}, bf16[1056,128]{1,0:T(8,128)(2,1)S(1)}, bf16[1056,128]{1,0:T(8,12...) custom-call(s32[1]{0:T(128)} %bitcast.pos_ref, f32[1]{0:T(128)S(6)} %copy.14.width_ref, ...), custom_call_target="tpu_custom_call" | custom-call | flops 1000000 | bytes 2000000 | tf_op jit(solution)/shard_map/span_groups/pallas_call | solution.py:162
  2.9 0.1 collective-permute-start.4
  3.0 2.0 %collective-permute-start.5 = (bf16[1056,128]{1,0:T(8,128)(2,1)S(1)}, bf16[1056,128]{1,0:T(8,128)(2,1)S(1)}, u32[]{:S(2)}, u32[]{:S(2)}) collective-permute-start(bf16[1056,128]{1,0:T(8,128)(2,1)S(1)} %get-tuple-element.50), channel_id=1, source_target_pairs={{0,64},{32,96},{64,0},{96,32},{1,65},{33,97},{65,1},{97,33},{2,66}... | collective-permute-start | bytes 811016 | tf_op jit(solution)/shard_map/ppermute | solution.py:567
  5.0 0.1 collective-permute-start.6
  5.0 1.9 %first_substep.1 = (f32[1944,128]{1,0:T(8,128)S(1)}, bf16[448,128]{1,0:T(8,128)(2,1)S(1)}, bf16[448,128]{1,0:T(8,128)(2,1)S(1)}, bf16[224,128]{1,0:T(8,128)(2,1)...) custom-call(s32[1]{0:T(128)} %bitcast.pos_ref, ...), custom_call_target="tpu_custom_call" | custom-call | flops 50000000 | bytes 3000000 | tf_op jit(solution)/shard_map/first_substep/pallas_call | solution.py:599
  6.9 0.2 collective-permute-start.2
  7.1 1.9 %collective-permute-start.3 = (bf16[224,128]{1,0:T(8,128)(2,1)S(1)}, bf16[224,128]{1,0:T(8,128)(2,1)S(1)}, u32[]{:S(2)}, u32[]{:S(2)}) collective-permute-start(bf16[224,128]{1,0:T(8,128)(2,1)S(1)} %get-tuple-element.46), channel_id=1, source_target_pairs={{0,30},{1,31},{2,0},{3,1},{4,2},{5,3},{6,4},{7,5},{8,6},{9,7},{10,... | collective-permute-start | bytes 172040 | tf_op jit(solution)/shard_map/ppermute | solution.py:563
  9.0 2.2 %collective-permute-done.2.refs_2_ = bf16[224,128]{1,0:T(8,128)(2,1)S(1)} collective-permute-done((bf16[224,128]{1,0:T(8,128)(2,1)S(1)}, bf16[224,128]{1,0:T(8,128)(2,1)S(1)}, u32[]{:S(2)}, u32[]{:S(2)}) %collective-permute-start.2) | collective-permute-done | bytes 57376 | tf_op jit(solution)/shard_map/ppermute | solution.py:563
  11.1 3.7 %collective-permute-start = (bf16[448,128]{1,0:T(8,128)(2,1)S(1)}, bf16[448,128]{1,0:T(8,128)(2,1)S(1)}, u32[]{:S(2)}, u32[]{:S(2)}) collective-permute-start(bf16[448,128]{1,0:T(8,128)(2,1)S(1)} %get-tuple-element.43.refs_4_), channel_id=1, source_target_pairs={{0,1},{1,2},{2,3},{3,4},{4,5},{5,6},{6,7},{7,8},{8,9},{9,10},{10,1... | collective-permute-start | bytes 344072 | tf_op jit(solution)/shard_map/ppermute | solution.py:563
  14.8 0.0 collective-permute-done.3.refs_3_
  14.8 1.5 %collective-permute-start.1 = (bf16[448,128]{1,0:T(8,128)(2,1)S(1)}, bf16[448,128]{1,0:T(8,128)(2,1)S(1)}, u32[]{:S(2)}, u32[]{:S(2)}) collective-permute-start(bf16[448,128]{1,0:T(8,128)(2,1)S(1)} %get-tuple-element.44.refs_5_), channel_id=1, source_target_pairs={{0,31},{1,0},{2,1},{3,2},{4,3},{5,4},{6,5},{7,6},{8,7},{9,8},{10,9... | collective-permute-start | bytes 344072 | tf_op jit(solution)/shard_map/ppermute | solution.py:563
  16.3 0.0 collective-permute-done.4.refs_1_
  16.3 0.0 collective-permute-done.5.refs_2_
  16.3 1.3 %collective-permute-done.6.refs_3_ = bf16[1056,128]{1,0:T(8,128)(2,1)S(1)} collective-permute-done((bf16[1056,128]{1,0:T(8,128)(2,1)S(1)}, bf16[1056,128]{1,0:T(8,128)(2,1)S(1)}, u32[]{:S(2)}, u32[]{:S(2)}) %collective-permute-start.6) | collective-permute-done | bytes 270368 | tf_op jit(solution)/shard_map/ppermute | solution.py:567
  17.6 4.8 %adjoint_forcing.1 = (bf16[528,128]{1,0:T(8,128)(2,1)S(1)}, bf16[528,128]{1,0:T(8,128)(2,1)S(1)}, bf16[528,128]{1,0:T(8,128)(2,1)S(1)}, bf16[528,128]{1,0:T(8,128)(2,1)S(1)}) custom-call(s32[1]{0:T(128)} %bitcast.pos_ref, f32[104,128]{1,0:T(8,128)S(1)} %get-tuple-element.41.shape_ref, bf16[1056,128]{1,0:T(8,128)(2,1)S(1)} %get-tuple-element.48.refs_0_, ...), custom_call_target="tpu_custom_call" | custom-call | flops 5000000000 | bytes 8000000 | tf_op jit(solution)/shard_map/adjoint_forcing/pallas_call | solution.py:274
  22.4 0.0 collective-permute-done.refs_0_
  22.4 3.6 %collective-permute-done.1.refs_1_ = bf16[448,128]{1,0:T(8,128)(2,1)S(1)} collective-permute-done((bf16[448,128]{1,0:T(8,128)(2,1)S(1)}, bf16[448,128]{1,0:T(8,128)(2,1)S(1)}, u32[]{:S(2)}, u32[]{:S(2)}) %collective-permute-start.1) | collective-permute-done | bytes 114720 | tf_op jit(solution)/shard_map/ppermute | solution.py:563
  26.0 0.0 collective-permute-start.7
  26.0 0.0 collective-permute-start.8
  26.0 1.9 %collective-permute-start.9 = (bf16[528,128]{1,0:T(8,128)(2,1)S(1)}, bf16[528,128]{1,0:T(8,128)(2,1)S(1)}, u32[]{:S(2)}, u32[]{:S(2)}) collective-permute-start(bf16[528,128]{1,0:T(8,128)(2,1)S(1)} %get-tuple-element.71), channel_id=1, source_target_pairs={{0,96},{32,64},{64,32},{96,0},{1,97},{33,65},{65,33},{97,1},{2,98}... | collective-permute-start | bytes 405512 | tf_op jit(solution)/shard_map/ppermute | solution.py:567
  27.9 0.2 first_join.1
  28.1 0.0 collective-permute-done.7.refs_1_
  28.1 4.3 %collective-permute-done.8.refs_2_ = bf16[528,128]{1,0:T(8,128)(2,1)S(1)} collective-permute-done((bf16[528,128]{1,0:T(8,128)(2,1)S(1)}, bf16[528,128]{1,0:T(8,128)(2,1)S(1)}, u32[]{:S(2)}, u32[]{:S(2)}) %collective-permute-start.8) | collective-permute-done | bytes 135200 | tf_op jit(solution)/shard_map/ppermute | solution.py:567
  32.4 2.1 %collective-permute-done.9.refs_3_ = bf16[528,128]{1,0:T(8,128)(2,1)S(1)} collective-permute-done((bf16[528,128]{1,0:T(8,128)(2,1)S(1)}, bf16[528,128]{1,0:T(8,128)(2,1)S(1)}, u32[]{:S(2)}, u32[]{:S(2)}) %collective-permute-start.9) | collective-permute-done | bytes 135200 | tf_op jit(solution)/shard_map/ppermute | solution.py:567
  34.5 1.6 %second_substep.1 = (f32[1944,128]{1,0:T(8,128)S(1)}, bf16[432,128]{1,0:T(8,128)(2,1)S(1)}, bf16[432,128]{1,0:T(8,128)(2,1)S(1)}, bf16[224,128]{1,0:T(8,128)(2,1)S(1)}, bf16[224,128]{1,0:T(8,128)(2,1)S(1)}) custom-call(s32[1]{0:T(128)} %bitcast.pos_ref, f32[104,128]{1,0:T(8,128)S(1)} %get-tuple-element.41.shape_ref, ...), custom_call_target="tpu_custom_call" | custom-call | flops 50000000 | bytes 4000000 | tf_op jit(solution)/shard_map/second_substep/pallas_call | solution.py:629
  36.1 2.5 %collective-permute-start.10 = (bf16[432,128]{1,0:T(8,128)(2,1)S(1)}, bf16[432,128]{1,0:T(8,128)(2,1)S(1)}, u32[]{:S(2)}, u32[]{:S(2)}) collective-permute-start(bf16[432,128]{1,0:T(8,128)(2,1)S(1)} %get-tuple-element.72.refs_4_), channel_id=1, source_target_pairs={{0,1},{1,2},{2,3},{3,4},{4,5},{5,6},{6,7},{7,8},{8,9},{9,10},{10,1... | collective-permute-start | bytes 331784 | tf_op jit(solution)/shard_map/ppermute | solution.py:563
  38.6 2.0 %collective-permute-start.11 = (bf16[432,128]{1,0:T(8,128)(2,1)S(1)}, bf16[432,128]{1,0:T(8,128)(2,1)S(1)}, u32[]{:S(2)}, u32[]{:S(2)}) collective-permute-start(bf16[432,128]{1,0:T(8,128)(2,1)S(1)} %get-tuple-element.73.refs_5_), channel_id=1, source_target_pairs={{0,31},{1,0},{2,1},{3,2},{4,3},{5,4},{6,5},{7,6},{8,7},{9,8},{10,9... | collective-permute-start | bytes 331784 | tf_op jit(solution)/shard_map/ppermute | solution.py:563
  40.6 5.2 %collective-permute-start.12 = (bf16[224,128]{1,0:T(8,128)(2,1)S(1)}, bf16[224,128]{1,0:T(8,128)(2,1)S(1)}, u32[]{:S(2)}, u32[]{:S(2)}) collective-permute-start(bf16[224,128]{1,0:T(8,128)(2,1)S(1)} %get-tuple-element.74), channel_id=1, source_target_pairs={{0,2},{1,3},{2,4},{3,5},{4,6},{5,7},{6,8},{7,9},{8,10},{9,11},{10,... | collective-permute-start | bytes 172040 | tf_op jit(solution)/shard_map/ppermute | solution.py:563
  45.9 0.0 collective-permute-start.13
  45.9 1.8 %collective-permute-done.12.refs_2_ = bf16[224,128]{1,0:T(8,128)(2,1)S(1)} collective-permute-done((bf16[224,128]{1,0:T(8,128)(2,1)S(1)}, bf16[224,128]{1,0:T(8,128)(2,1)S(1)}, u32[]{:S(2)}, u32[]{:S(2)}) %collective-permute-start.12) | collective-permute-done | bytes 57376 | tf_op jit(solution)/shard_map/ppermute | solution.py:563
  47.7 5.7 %collective-permute-done.13.refs_3_ = bf16[224,128]{1,0:T(8,128)(2,1)S(1)} collective-permute-done((bf16[224,128]{1,0:T(8,128)(2,1)S(1)}, bf16[224,128]{1,0:T(8,128)(2,1)S(1)}, u32[]{:S(2)}, u32[]{:S(2)}) %collective-permute-start.13) | collective-permute-done | bytes 57376 | tf_op jit(solution)/shard_map/ppermute | solution.py:563
  53.4 0.0 collective-permute-done.10.refs_0_
  53.4 0.0 collective-permute-done.11.refs_1_
  53.4 1.1 %second_join.1 = (bf16[1944,128]{1,0:T(8,128)(2,1)}, f32[9,1,128]{2,1,0:T(1,128)}) custom-call(f32[104,128]{1,0:T(8,128)S(1)} %get-tuple-element.41.shape_ref, bf16[432,128]{1,0:T(8,128)(2,1)S(1)} %collective-permute-done.10.refs_0_, bf16[432,128]{1,0:T(8,128)(2,1)S(1)} %collective-permute-done.11.refs_1_, ...), custom_call_target="tpu_custom_call" | custom-call | flops 10000000 | bytes 3000000 | tf_op jit(solution)/shard_map/second_join/pallas_call | solution.py:641
Async XLA Ops:
  2.9 13.4 %collective-permute-start.4 = (bf16[1056,128]{1,0:T(8,128)(2,1)S(1)}, bf16[1056,128]{1,0:T(8,128)(2,1)S(1)}, u32[]{:S(2)}, u32[]{:S(2)}) collective-permute-start(bf16[1056,128]{1,0:T(8,128)(2,1)S(1)} %get-tuple-element.49), channel_id=1, source_target_pairs={{0,32},{32,0},{64,96},{96,64},{1,33},{33,1},{65,97},{97,65},{2,34}... | collective-permute-start | bytes 811016 | tf_op jit(solution)/shard_map/ppermute | solution.py:567
  3.0 13.3 %collective-permute-start.5 = (bf16[1056,128]{1,0:T(8,128)(2,1)S(1)}, bf16[1056,128]{1,0:T(8,128)(2,1)S(1)}, u32[]{:S(2)}, u32[]{:S(2)}) collective-permute-start(bf16[1056,128]{1,0:T(8,128)(2,1)S(1)} %get-tuple-element.50), channel_id=1, source_target_pairs={{0,64},{32,96},{64,0},{96,32},{1,65},{33,97},{65,1},{97,33},{2,66}... | collective-permute-start | bytes 811016 | tf_op jit(solution)/shard_map/ppermute | solution.py:567
  5.0 12.6 %collective-permute-start.6 = (bf16[1056,128]{1,0:T(8,128)(2,1)S(1)}, bf16[1056,128]{1,0:T(8,128)(2,1)S(1)}, u32[]{:S(2)}, u32[]{:S(2)}) collective-permute-start(bf16[1056,128]{1,0:T(8,128)(2,1)S(1)} %get-tuple-element.51), channel_id=1, source_target_pairs={{0,96},{32,64},{64,32},{96,0},{1,97},{33,65},{65,33},{97,1},{2,98}... | collective-permute-start | bytes 811016 | tf_op jit(solution)/shard_map/ppermute | solution.py:567
  6.9 4.2 %collective-permute-start.2 = (bf16[224,128]{1,0:T(8,128)(2,1)S(1)}, bf16[224,128]{1,0:T(8,128)(2,1)S(1)}, u32[]{:S(2)}, u32[]{:S(2)}) collective-permute-start(bf16[224,128]{1,0:T(8,128)(2,1)S(1)} %get-tuple-element.45), channel_id=1, source_target_pairs={{0,2},{1,3},{2,4},{3,5},{4,6},{5,7},{6,8},{7,9},{8,10},{9,11},{10,... | collective-permute-start | bytes 172040 | tf_op jit(solution)/shard_map/ppermute | solution.py:563
  7.1 7.7 %collective-permute-start.3 = (bf16[224,128]{1,0:T(8,128)(2,1)S(1)}, bf16[224,128]{1,0:T(8,128)(2,1)S(1)}, u32[]{:S(2)}, u32[]{:S(2)}) collective-permute-start(bf16[224,128]{1,0:T(8,128)(2,1)S(1)} %get-tuple-element.46), channel_id=1, source_target_pairs={{0,30},{1,31},{2,0},{3,1},{4,2},{5,3},{6,4},{7,5},{8,6},{9,7},{10,... | collective-permute-start | bytes 172040 | tf_op jit(solution)/shard_map/ppermute | solution.py:563
  11.1 11.3 %collective-permute-start = (bf16[448,128]{1,0:T(8,128)(2,1)S(1)}, bf16[448,128]{1,0:T(8,128)(2,1)S(1)}, u32[]{:S(2)}, u32[]{:S(2)}) collective-permute-start(bf16[448,128]{1,0:T(8,128)(2,1)S(1)} %get-tuple-element.43.refs_4_), channel_id=1, source_target_pairs={{0,1},{1,2},{2,3},{3,4},{4,5},{5,6},{6,7},{7,8},{8,9},{9,10},{10,1... | collective-permute-start | bytes 344072 | tf_op jit(solution)/shard_map/ppermute | solution.py:563
  14.8 11.2 %collective-permute-start.1 = (bf16[448,128]{1,0:T(8,128)(2,1)S(1)}, bf16[448,128]{1,0:T(8,128)(2,1)S(1)}, u32[]{:S(2)}, u32[]{:S(2)}) collective-permute-start(bf16[448,128]{1,0:T(8,128)(2,1)S(1)} %get-tuple-element.44.refs_5_), channel_id=1, source_target_pairs={{0,31},{1,0},{2,1},{3,2},{4,3},{5,4},{6,5},{7,6},{8,7},{9,8},{10,9... | collective-permute-start | bytes 344072 | tf_op jit(solution)/shard_map/ppermute | solution.py:563
  26.0 2.1 %collective-permute-start.7 = (bf16[528,128]{1,0:T(8,128)(2,1)S(1)}, bf16[528,128]{1,0:T(8,128)(2,1)S(1)}, u32[]{:S(2)}, u32[]{:S(2)}) collective-permute-start(bf16[528,128]{1,0:T(8,128)(2,1)S(1)} %get-tuple-element.69), channel_id=1, source_target_pairs={{0,32},{32,0},{64,96},{96,64},{1,33},{33,1},{65,97},{97,65},{2,34}... | collective-permute-start | bytes 405512 | tf_op jit(solution)/shard_map/ppermute | solution.py:567
  26.0 6.4 %collective-permute-start.8 = (bf16[528,128]{1,0:T(8,128)(2,1)S(1)}, bf16[528,128]{1,0:T(8,128)(2,1)S(1)}, u32[]{:S(2)}, u32[]{:S(2)}) collective-permute-start(bf16[528,128]{1,0:T(8,128)(2,1)S(1)} %get-tuple-element.70), channel_id=1, source_target_pairs={{0,64},{32,96},{64,0},{96,32},{1,65},{33,97},{65,1},{97,33},{2,66}... | collective-permute-start | bytes 405512 | tf_op jit(solution)/shard_map/ppermute | solution.py:567
  26.0 8.5 %collective-permute-start.9 = (bf16[528,128]{1,0:T(8,128)(2,1)S(1)}, bf16[528,128]{1,0:T(8,128)(2,1)S(1)}, u32[]{:S(2)}, u32[]{:S(2)}) collective-permute-start(bf16[528,128]{1,0:T(8,128)(2,1)S(1)} %get-tuple-element.71), channel_id=1, source_target_pairs={{0,96},{32,64},{64,32},{96,0},{1,97},{33,65},{65,33},{97,1},{2,98}... | collective-permute-start | bytes 405512 | tf_op jit(solution)/shard_map/ppermute | solution.py:567
  36.1 17.2 %collective-permute-start.10 = (bf16[432,128]{1,0:T(8,128)(2,1)S(1)}, bf16[432,128]{1,0:T(8,128)(2,1)S(1)}, u32[]{:S(2)}, u32[]{:S(2)}) collective-permute-start(bf16[432,128]{1,0:T(8,128)(2,1)S(1)} %get-tuple-element.72.refs_4_), channel_id=1, source_target_pairs={{0,1},{1,2},{2,3},{3,4},{4,5},{5,6},{6,7},{7,8},{8,9},{9,10},{10,1... | collective-permute-start | bytes 331784 | tf_op jit(solution)/shard_map/ppermute | solution.py:563
  38.6 14.7 %collective-permute-start.11 = (bf16[432,128]{1,0:T(8,128)(2,1)S(1)}, bf16[432,128]{1,0:T(8,128)(2,1)S(1)}, u32[]{:S(2)}, u32[]{:S(2)}) collective-permute-start(bf16[432,128]{1,0:T(8,128)(2,1)S(1)} %get-tuple-element.73.refs_5_), channel_id=1, source_target_pairs={{0,31},{1,0},{2,1},{3,2},{4,3},{5,4},{6,5},{7,6},{8,7},{9,8},{10,9... | collective-permute-start | bytes 331784 | tf_op jit(solution)/shard_map/ppermute | solution.py:563
  40.6 7.1 %collective-permute-start.12 = (bf16[224,128]{1,0:T(8,128)(2,1)S(1)}, bf16[224,128]{1,0:T(8,128)(2,1)S(1)}, u32[]{:S(2)}, u32[]{:S(2)}) collective-permute-start(bf16[224,128]{1,0:T(8,128)(2,1)S(1)} %get-tuple-element.74), channel_id=1, source_target_pairs={{0,2},{1,3},{2,4},{3,5},{4,6},{5,7},{6,8},{7,9},{8,10},{9,11},{10,... | collective-permute-start | bytes 172040 | tf_op jit(solution)/shard_map/ppermute | solution.py:563
  45.9 7.5 %collective-permute-start.13 = (bf16[224,128]{1,0:T(8,128)(2,1)S(1)}, bf16[224,128]{1,0:T(8,128)(2,1)S(1)}, u32[]{:S(2)}, u32[]{:S(2)}) collective-permute-start(bf16[224,128]{1,0:T(8,128)(2,1)S(1)} %get-tuple-element.75), channel_id=1, source_target_pairs={{0,30},{1,31},{2,0},{3,1},{4,2},{5,3},{6,4},{7,5},{8,6},{9,7},{10,... | collective-permute-start | bytes 172040 | tf_op jit(solution)/shard_map/ppermute | solution.py:563

commit v2 on v1

--- a/solution.py
+++ b/solution.py
@@ -75,8 +75,9 @@
         both[0, layer, :PLANE, layer, :PLANE] = radial
         both[1, layer, :PLANE, layer, :PLANE] = around
     high, low = halves(both.reshape(4 * PAD, 2 * PAD))
-    slope = np.concatenate([high, low, high], axis=1)
-    return synthesis.astype(jnp.bfloat16), halves(wave), slope, halves(analysis)
+    slope = np.concatenate([high, low], axis=1)
+    kinds = [table.astype(jnp.bfloat16) for table in (synthesis, wave, analysis)]
+    return kinds[0], kinds[1], slope, kinds[2]
 
 
 def smem():
@@ -109,8 +110,10 @@
 
 
 def repack_kernel(pos_ref, width_ref, adj_hbm, fwd_hbm, height_hbm, mask_hbm, *refs):
-    groups, wide_adj, shape_ref = refs[0:4], refs[4], refs[5]
-    adj_ref, fwd_ref, wide_fwd, height_ref, mask_ref, sems = refs[6:12]
+    shared, adj_single, fwd_single = refs[0:2], refs[2:4], refs[4:6]
+    wide_adj, shape_ref = refs[6:8]
+    adj_ref, fwd_ref, wide_fwd, height_ref, mask_ref, sems = refs[8:14]
+    singles = (adj_single, fwd_single)
     pairs = (
         (adj_hbm, adj_ref),
         (fwd_hbm, fwd_ref),
@@ -128,7 +131,7 @@
     for which, (x_ref, wide) in enumerate(((adj_ref, wide_adj), (fwd_ref, wide_fwd))):
         copies[which].wait()
         wide[pl.ds(0, POINTS), :] = x_ref[...].astype(F32)
-        for flip, out in enumerate(groups):
+        for flip, out in enumerate((*shared, *singles[which])):
             group = pos ^ flip
             for comp in range(3):
                 parts = []
@@ -137,7 +140,7 @@
                     rows = wide[pl.ds(start, PAD, stride=8), :]
                     parts.append(jnp.where(keep, rows, 0.0))
                 block = jnp.concatenate(parts, axis=0).astype(BF16)
-                at = which * ROWS + comp * 2 * PAD
+                at = comp * 2 * PAD + (which * ROWS if flip < 2 else 0)
                 out[at : at + 2 * PAD, :] = block
     for copy in copies[2:]:
         copy.wait()
@@ -162,7 +165,8 @@
     return call(
         repack_kernel,
         "span_groups",
-        [((2 * ROWS, 128), BF16)] * 4
+        [((2 * ROWS, 128), BF16)] * 2
+        + [((ROWS, 128), BF16)] * 4
         + [((POINTS + 56, 128), F32), ((32 + 8 * NODES, 128), F32)],
         [
             pltpu.VMEM((POINTS, 128), BF16),
@@ -184,32 +188,31 @@
     return jnp.concatenate(parts, axis=0)
 
 
-def transform(pos, which, chunks, tables, planes, zplanes, grads):
-    synth_ref, wave_hi_ref, wave_lo_ref, slope_ref = tables
+def transform(pos, which, shared, single, tables, planes, zplanes, grads):
+    synth_ref, wave_ref, slope_ref = tables
     rows = slice(which * ROWS, (which + 1) * ROWS)
-    modes = jnp.concatenate([chunk[rows, :] for chunk in chunks], axis=1)
+    parts = [chunk[rows, :] for chunk in shared] + [chunk[...] for chunk in single]
+    modes = jnp.concatenate(parts, axis=1)
     planes[...] = jnp.dot(modes, gather(synth_ref, pos), preferred_element_type=F32)
-    zplanes[...] = jnp.dot(
-        modes, gather(wave_hi_ref, pos), preferred_element_type=F32
-    ) + jnp.dot(modes, gather(wave_lo_ref, pos), preferred_element_type=F32)
+    zplanes[...] = jnp.dot(modes, gather(wave_ref, pos), preferred_element_type=F32)
     slope = slope_ref[...]
     for comp in range(3):
-        block = planes[comp * 2 * PAD : (comp + 1) * 2 * PAD, :]
-        high = block.astype(BF16)
-        low = (block - high.astype(F32)).astype(BF16)
-        stack = jnp.concatenate([high, high, low], axis=0)
+        block = planes[comp * 2 * PAD : (comp + 1) * 2 * PAD, :].astype(BF16)
+        stack = jnp.concatenate([block, block], axis=0)
         grads[comp] = jnp.dot(slope, stack, preferred_element_type=F32)
 
 
+def adj_kernel(pos_ref, *refs):
+    transform(pos_ref[0], 0, refs[0:2], refs[2:4], refs[4:7], *refs[7:10])
+
+
 def force_kernel(pos_ref, shape_ref, *refs):
-    chunks, tables = refs[0:4], refs[4:10]
-    outs = refs[10:14]
-    adj_planes, adj_zplanes, adj_grads = refs[14:17]
-    fwd_planes, fwd_zplanes, fwd_grads, force = refs[17:21]
-    an_hi_ref, an_lo_ref = tables[4:]
+    tables, an_ref = refs[4:7], refs[7]
+    adj_planes, adj_zplanes, adj_grads = refs[8:11]
+    outs = refs[11:15]
+    fwd_planes, fwd_zplanes, fwd_grads, force = refs[15:19]
     pos = pos_ref[0]
-    transform(pos, 0, chunks, tables[:4], adj_planes, adj_zplanes, adj_grads)
-    transform(pos, 1, chunks, tables[:4], fwd_planes, fwd_zplanes, fwd_grads)
+    transform(pos, 1, refs[0:2], refs[2:4], tables, fwd_planes, fwd_zplanes, fwd_grads)
     planes, zplanes = (fwd_planes, adj_planes), (fwd_zplanes, adj_zplanes)
     grads = (fwd_grads, adj_grads)
 
@@ -252,14 +255,13 @@
     def pick(ref):
         return jnp.concatenate([ref[pos ^ flip] for flip in range(4)], axis=1)
 
-    an_hi, an_lo = pick(an_hi_ref), pick(an_lo_ref)
+    analysis = pick(an_ref)
     total = force[...]
     high = total.astype(BF16)
     low = (total - high.astype(F32)).astype(BF16)
     result = (
-        jnp.dot(high, an_hi, preferred_element_type=F32)
-        + jnp.dot(low, an_hi, preferred_element_type=F32)
-        + jnp.dot(high, an_lo, preferred_element_type=F32)
+        jnp.dot(high, analysis, preferred_element_type=F32)
+        + jnp.dot(low, analysis, preferred_element_type=F32)
     ).astype(BF16)
     for flip, out in enumerate(outs):
         out[...] = result[:, 128 * flip : 128 * (flip + 1)]
@@ -269,18 +271,30 @@
     return [(ROWS, NK), (ROWS, NK), (3, 4 * PAD, NK)]
 
 
-def forcing(pos, shape, chunks, tables):
-    fields = [pltpu.VMEM(shape, F32) for shape in plane_shapes()]
+def adj_side(pos, shared, single, tables):
+    return call(
+        adj_kernel,
+        "adjoint_planes",
+        [(shape, F32) for shape in plane_shapes()],
+        [],
+        [smem()] + [vmem()] * 7,
+        1_500_000_000,
+        8_000_000,
+        12,
+    )(pos, *shared, *single, *tables)
+
+
+def forcing(pos, shape, shared, single, tables, adj_fields):
     return call(
         force_kernel,
         "adjoint_forcing",
         [((ROWS, 128), BF16)] * 4,
-        fields + fields + [pltpu.VMEM((ROWS, NK), F32)],
-        [smem()] + [vmem()] * 11,
-        5_000_000_000,
+        [pltpu.VMEM(dims, F32) for dims in plane_shapes()] + [pltpu.VMEM((ROWS, NK), F32)],
+        [smem()] + [vmem()] * 12,
+        2_500_000_000,
         8_000_000,
         20,
-    )(pos, shape, *chunks, *tables)
+    )(pos, shape, *shared, *single, *tables, *adj_fields)
 
 
 def mirror(matrix):
@@ -421,9 +435,9 @@
 
 
 def first_kernel(pos_ref, shape_ref, wide, *refs):
-    given, refs = refs[0:6], refs[6:]
+    given, refs = refs[0:4], refs[4:]
     out, right, left, right_far, left_far = refs[0:5]
-    tables, (visc, faces, sems) = refs[5:11], refs[11:14]
+    tables, (visc, faces, sems) = refs[5:9], refs[9:12]
     copies = [
         pltpu.make_async_copy(source, target, sems.at[n])
         for n, (source, target) in enumerate(zip(given, tables))
@@ -572,12 +586,9 @@
 
 
 def local(fwd_modes, adj_modes, layer_height, column_width, wall_mask):
-    synth, (wave_hi, wave_lo), slope, (an_hi, an_lo) = plane_tables()
-    split = lambda table: table.reshape(NK, 4, 128).transpose(1, 0, 2)
-    constants = [
-        jnp.asarray(table)
-        for table in (synth, wave_hi, wave_lo, slope, split(an_hi), split(an_lo))
-    ]
+    synth, wave, slope, analysis = plane_tables()
+    analysis = analysis.reshape(NK, 4, 128).transpose(1, 0, 2)
+    constants = [jnp.asarray(table) for table in (synth, wave, slope, analysis)]
     pos = lax.axis_index("span").astype(jnp.int32).reshape(1)
 
     def resident(field):
@@ -591,10 +602,11 @@
     def exchange(parts):
         return [parts[0]] + [swap(part, flip + 1) for flip, part in enumerate(parts[1:])]
 
-    *groups, adj_wide, shape = repack(
+    own, sibling, adj_2, adj_3, fwd_2, fwd_3, adj_wide, shape = repack(
         pos, adj_flat, fwd_flat, layer_height, column_width, wall_mask
     )
-    chunks = exchange(groups)
+    shared = [own, swap(sibling, 1)]
+    adj_away, fwd_away = [swap(adj_2, 2), swap(adj_3, 3)], [swap(fwd_2, 2), swap(fwd_3, 3)]
 
     state, right, left, right_far, left_far, *tables = call(
         first_kernel,
@@ -603,17 +615,22 @@
         + [((16 * COLS + 16, 128), BF16)] * 2
         + far_shapes
         + [(table.shape, BF16) for table in constants],
-        work + [pltpu.SemaphoreType.DMA((6,))],
-        [smem()] + [vmem()] * 2 + [hbm()] * 6,
+        work + [pltpu.SemaphoreType.DMA((4,))],
+        [smem()] + [vmem()] * 2 + [hbm()] * 4,
         50_000_000,
         3_000_000,
         10,
     )(pos, shape, adj_wide, *map(in_hbm, constants))
-    near, far = halo(right, left, 1), halo(right_far, left_far, 2)
-    *far, chunks[0] = lax.optimization_barrier((*far, chunks[0]))
-    parts = forcing(pos, shape, chunks, tables)
-    *near, parts = lax.optimization_barrier((*near, tuple(parts)))
+    near_right, near_left, *adj_away = lax.optimization_barrier((right, left, *adj_away))
+    near = halo(near_right, near_left, 1)
+    adj_fields = adj_side(pos, shared, adj_away, tables[:3])
+    parts = forcing(pos, shape, shared, fwd_away, tables, adj_fields)
+    parts = list(parts)
+    right_far, left_far, *near, parts[0] = lax.optimization_barrier(
+        (right_far, left_far, *near, parts[0])
+    )
     parts = exchange(parts)
+    far = halo(right_far, left_far, 2)
 
     base, sides = call(
         first_join_kernel,

time: 54.6 us -> 52.1 us (0.954)
  Pallas kernels: 11.1 us -> 9.43 us
    ppermute x6 -> x8, waiting for transfers between devices: 7.68 us -> 3.57 us  [swap(): lax.ppermute(value, 'span', [(n, n ^ flip) for n in range(lax.axis_size('...]
    ppermute x8, waiting for transfers between devices: 13.3 us -> 16.9 us  [ring(): lax.ppermute(value, 'xsec', [(n, (n + shift) % count) for n in range(coun...]
    ppermute x8, starting transfers between devices: 17 us -> 14.3 us  [ring(): lax.ppermute(value, 'xsec', [(n, (n + shift) % count) for n in range(coun...]
    ppermute x6 -> x8, starting transfers between devices: 4 us -> 6.29 us  [swap(): lax.ppermute(value, 'span', [(n, n ^ flip) for n in range(lax.axis_size('...]
    pallas_call x2 -> x3, Pallas kernels: 6.4 us -> 5.12 us  [the longest x1 2.25 us: forcing(): call(force_kernel, 'adjoint_forcing', [((ROWS, 128), BF16)] * 4, [pltpu.V...]
  transfers between devices with their start and end apart: 14 -> 16, of which waited for: 7 -> 7; matrix products, arithmetic and copies ran while one was open for 0% -> 0% of each run, Pallas kernels for 13% -> 10%
where the time goes in v2:
time: 52.1 us; the launch traced here: 51.9 us
  starting transfers between devices  20.6 us (40%)
  waiting for transfers between devices  20.5 us (39%)
  Pallas kernels  9.43 us (18%)
  between operations  1.37 us (3%)
    ppermute x8, waiting for transfers between devices, ring(): lax.ppermute(value, 'xsec', [(n, (n + shift) % count) for n in range(coun...  16.9 us
    ppermute x8, starting transfers between devices, ring(): lax.ppermute(value, 'xsec', [(n, (n + shift) % count) for n in range(coun...  14.3 us
    ppermute x8, starting transfers between devices, swap(): lax.ppermute(value, 'span', [(n, n ^ flip) for n in range(lax.axis_size('...  6.29 us
    ppermute x8, waiting for transfers between devices, swap(): lax.ppermute(value, 'span', [(n, n ^ flip) for n in range(lax.axis_size('...  3.57 us
    pallas_call x1, Pallas kernels, forcing(): call(force_kernel, 'adjoint_forcing', [((ROWS, 128), BF16)] * 4, [pltpu.V...  2.25 us
    pallas_call x1, Pallas kernels, repack(): call(repack_kernel, 'span_groups', [((2 * ROWS, 128), BF16)] * 2 + [((ROW...  1.58 us
    pallas_call x1, Pallas kernels, local(): call(second_kernel, 'second_substep', [state_shape] + [((16 * COLS, 128),...  1.57 us
    pallas_call x1, Pallas kernels, local(): call(first_kernel, 'first_substep', [state_shape] + [((16 * COLS + 16, 12...  1.47 us
  transfers between devices with their start and end apart: 16, of which 7 were waited for; matrix products, arithmetic and copies ran while one was open for 0% of the time, Pallas kernels for 10%

profile of v2, /device:TPU:30, one launch (start us, length us, event | category | flops | bytes accessed | tf_op | source)
XLA Modules:
  0.0 51.9 jit_solution(12026426736953116889)
XLA Ops:
  1.3 1.6 %span_groups.1 = (bf16[1056,128]{1,0:T(8,128)(2,1)S(1)}, bf16[1056,128]{1,0:T(8,128)(2,1)S(1)}, bf16[528,128]{1,0:T(8,128)(2,1)S(1)}, bf16[528,128]{1,0:T(8,128)...) custom-call(s32[1]{0:T(128)} %bitcast.pos_ref, ...), custom_call_target="tpu_custom_call" | custom-call | flops 1000000 | bytes 2000000 | tf_op jit(solution)/shard_map/span_groups/pallas_call | solution.py:165
  2.9 0.1 collective-permute-start.4
  3.0 2.0 %collective-permute-start = (bf16[528,128]{1,0:T(8,128)(2,1)S(1)}, bf16[528,128]{1,0:T(8,128)(2,1)S(1)}, u32[]{:S(2)}, u32[]{:S(2)}) collective-permute-start(bf16[528,128]{1,0:T(8,128)(2,1)S(1)} %get-tuple-element.50), channel_id=1, source_target_pairs={{0,64},{32,96},{64,0},{96,32},{1,65},{33,97},{65,1},{97,33},{2,66}... | collective-permute-start | bytes 405512 | tf_op jit(solution)/shard_map/ppermute | solution.py:581
  5.0 0.1 collective-permute-start.1
  5.0 1.7 %collective-permute-start.5 = (bf16[528,128]{1,0:T(8,128)(2,1)S(1)}, bf16[528,128]{1,0:T(8,128)(2,1)S(1)}, u32[]{:S(2)}, u32[]{:S(2)}) collective-permute-start(bf16[528,128]{1,0:T(8,128)(2,1)S(1)} %get-tuple-element.56), channel_id=1, source_target_pairs={{0,64},{32,96},{64,0},{96,32},{1,65},{33,97},{65,1},{97,33},{2,66}... | collective-permute-start | bytes 405512 | tf_op jit(solution)/shard_map/ppermute | solution.py:581
  6.8 0.0 collective-permute-start.6
  6.8 1.5 %first_substep.1 = (f32[1944,128]{1,0:T(8,128)S(1)}, bf16[448,128]{1,0:T(8,128)(2,1)S(1)}, bf16[448,128]{1,0:T(8,128)(2,1)S(1)}, bf16[224,128]{1,0:T(8,128)(2,1)...) custom-call(s32[1]{0:T(128)} %bitcast.pos_ref, ...), custom_call_target="tpu_custom_call" | custom-call | flops 50000000 | bytes 3000000 | tf_op jit(solution)/shard_map/first_substep/pallas_call | solution.py:611
  8.2 1.2 %collective-permute-done.refs_2_ = bf16[528,128]{1,0:T(8,128)(2,1)S(1)} collective-permute-done((bf16[528,128]{1,0:T(8,128)(2,1)S(1)}, bf16[528,128]{1,0:T(8,128)(2,1)S(1)}, u32[]{:S(2)}, u32[]{:S(2)}) %collective-permute-start) | collective-permute-done | bytes 135200 | tf_op jit(solution)/shard_map/ppermute | solution.py:581
  9.4 2.4 %collective-permute-done.1.refs_3_ = bf16[528,128]{1,0:T(8,128)(2,1)S(1)} collective-permute-done((bf16[528,128]{1,0:T(8,128)(2,1)S(1)}, bf16[528,128]{1,0:T(8,128)(2,1)S(1)}, u32[]{:S(2)}, u32[]{:S(2)}) %collective-permute-start.1) | collective-permute-done | bytes 135200 | tf_op jit(solution)/shard_map/ppermute | solution.py:581
  11.8 3.6 %collective-permute-start.2 = (bf16[448,128]{1,0:T(8,128)(2,1)S(1)}, bf16[448,128]{1,0:T(8,128)(2,1)S(1)}, u32[]{:S(2)}, u32[]{:S(2)}) collective-permute-start(bf16[448,128]{1,0:T(8,128)(2,1)S(1)} %get-tuple-element.52.refs_4_), channel_id=1, source_target_pairs={{0,1},{1,2},{2,3},{3,4},{4,5},{5,6},{6,7},{7,8},{8,9},{9,10},{10,1... | collective-permute-start | bytes 344072 | tf_op jit(solution)/shard_map/ppermute | solution.py:577
  15.3 0.9 %collective-permute-start.3 = (bf16[448,128]{1,0:T(8,128)(2,1)S(1)}, bf16[448,128]{1,0:T(8,128)(2,1)S(1)}, u32[]{:S(2)}, u32[]{:S(2)}) collective-permute-start(bf16[448,128]{1,0:T(8,128)(2,1)S(1)} %get-tuple-element.53.refs_5_), channel_id=1, source_target_pairs={{0,31},{1,0},{2,1},{3,2},{4,3},{5,4},{6,5},{7,6},{8,7},{9,8},{10,9... | collective-permute-start | bytes 344072 | tf_op jit(solution)/shard_map/ppermute | solution.py:577
  16.2 0.0 collective-permute-done.4.refs_1_
  16.2 1.3 %adjoint_planes.1 = (f32[528,512]{1,0:T(8,128)S(1)}, f32[528,512]{1,0:T(8,128)S(1)}, f32[3,352,512]{2,1,0:T(8,128)S(1)}) custom-call(s32[1]{0:T(128)} %bitcast.pos_ref, bf16[1056,128]{1,0:T(8,128)(2,1)S(1)} %get-tuple-element.54.refs_0_, bf16[1056,128]{1,0:T(8,128)(2,1)S(1)} %collective-permute-done.4.refs_1_, ...), custom_call_target="tpu_custom_call" | custom-call | flops 1500000000 | bytes 8000000 | tf_op jit(solution)/shard_map/adjoint_planes/pallas_call | solution.py:275
  17.5 0.0 collective-permute-done.5.refs_2_
  17.5 0.0 collective-permute-done.6.refs_3_
  17.6 2.2 %adjoint_forcing.1 = (bf16[528,128]{1,0:T(8,128)(2,1)S(1)}, bf16[528,128]{1,0:T(8,128)(2,1)S(1)}, bf16[528,128]{1,0:T(8,128)(2,1)S(1)}, bf16[528,128]{1,0:T(8,128)(2,1)S(1)}) custom-call(s32[1]{0:T(128)} %bitcast.pos_ref, f32[104,128]{1,0:T(8,128)S(1)} %get-tuple-element.44.shape_ref, bf16[1056,128]{1,0:T(8,128)(2,1)S(1)} %get-tuple-element.54.refs_0_, ...), custom_call_target="tpu_custom_call" | custom-call | flops 2500000000 | bytes 8000000 | tf_op jit(solution)/shard_map/adjoint_forcing/pallas_call | solution.py:288
  19.8 1.6 %collective-permute-start.10 = (bf16[528,128]{1,0:T(8,128)(2,1)S(1)}, bf16[528,128]{1,0:T(8,128)(2,1)S(1)}, u32[]{:S(2)}, u32[]{:S(2)}) collective-permute-start(bf16[528,128]{1,0:T(8,128)(2,1)S(1)} %get-tuple-element.76), channel_id=1, source_target_pairs={{0,64},{32,96},{64,0},{96,32},{1,65},{33,97},{65,1},{97,33},{2,66}... | collective-permute-start | bytes 405512 | tf_op jit(solution)/shard_map/ppermute | solution.py:581
  21.4 0.8 %collective-permute-start.11 = (bf16[528,128]{1,0:T(8,128)(2,1)S(1)}, bf16[528,128]{1,0:T(8,128)(2,1)S(1)}, u32[]{:S(2)}, u32[]{:S(2)}) collective-permute-start(bf16[528,128]{1,0:T(8,128)(2,1)S(1)} %get-tuple-element.77), channel_id=1, source_target_pairs={{0,96},{32,64},{64,32},{96,0},{1,97},{33,65},{65,33},{97,1},{2,98}... | collective-permute-start | bytes 405512 | tf_op jit(solution)/shard_map/ppermute | solution.py:581
  22.2 0.0 collective-permute-start.9
  22.2 0.0 collective-permute-done.2.refs_0_
  22.2 3.8 %collective-permute-done.3.refs_1_ = bf16[448,128]{1,0:T(8,128)(2,1)S(1)} collective-permute-done((bf16[448,128]{1,0:T(8,128)(2,1)S(1)}, bf16[448,128]{1,0:T(8,128)(2,1)S(1)}, u32[]{:S(2)}, u32[]{:S(2)}) %collective-permute-start.3) | collective-permute-done | bytes 114720 | tf_op jit(solution)/shard_map/ppermute | solution.py:577
  26.0 0.1 collective-permute-start.7
  26.2 1.9 %collective-permute-start.8 = (bf16[224,128]{1,0:T(8,128)(2,1)S(1)}, bf16[224,128]{1,0:T(8,128)(2,1)S(1)}, u32[]{:S(2)}, u32[]{:S(2)}) collective-permute-start(bf16[224,128]{1,0:T(8,128)(2,1)S(1)} %get-tuple-element.71), channel_id=1, source_target_pairs={{0,30},{1,31},{2,0},{3,1},{4,2},{5,3},{6,4},{7,5},{8,6},{9,7},{10,... | collective-permute-start | bytes 172040 | tf_op jit(solution)/shard_map/ppermute | solution.py:577
  28.1 2.2 %collective-permute-done.7.refs_2_ = bf16[224,128]{1,0:T(8,128)(2,1)S(1)} collective-permute-done((bf16[224,128]{1,0:T(8,128)(2,1)S(1)}, bf16[224,128]{1,0:T(8,128)(2,1)S(1)}, u32[]{:S(2)}, u32[]{:S(2)}) %collective-permute-start.7) | collective-permute-done | bytes 57376 | tf_op jit(solution)/shard_map/ppermute | solution.py:577
  30.2 3.5 %collective-permute-done.8.refs_3_ = bf16[224,128]{1,0:T(8,128)(2,1)S(1)} collective-permute-done((bf16[224,128]{1,0:T(8,128)(2,1)S(1)}, bf16[224,128]{1,0:T(8,128)(2,1)S(1)}, u32[]{:S(2)}, u32[]{:S(2)}) %collective-permute-start.8) | collective-permute-done | bytes 57376 | tf_op jit(solution)/shard_map/ppermute | solution.py:577
  33.7 0.2 first_join.1
  33.9 0.0 collective-permute-done.10.refs_2_
  33.9 0.0 collective-permute-done.11.refs_3_
  33.9 0.0 collective-permute-done.9.refs_1_
  33.9 1.6 %second_substep.1 = (f32[1944,128]{1,0:T(8,128)S(1)}, bf16[432,128]{1,0:T(8,128)(2,1)S(1)}, bf16[432,128]{1,0:T(8,128)(2,1)S(1)}, bf16[224,128]{1,0:T(8,128)(2,1)S(1)}, bf16[224,128]{1,0:T(8,128)(2,1)S(1)}) custom-call(s32[1]{0:T(128)} %bitcast.pos_ref, f32[104,128]{1,0:T(8,128)S(1)} %get-tuple-element.44.shape_ref, ...), custom_call_target="tpu_custom_call" | custom-call | flops 50000000 | bytes 4000000 | tf_op jit(solution)/shard_map/second_substep/pallas_call | solution.py:646
  35.5 2.4 %collective-permute-start.12 = (bf16[432,128]{1,0:T(8,128)(2,1)S(1)}, bf16[432,128]{1,0:T(8,128)(2,1)S(1)}, u32[]{:S(2)}, u32[]{:S(2)}) collective-permute-start(bf16[432,128]{1,0:T(8,128)(2,1)S(1)} %get-tuple-element.78.refs_4_), channel_id=1, source_target_pairs={{0,1},{1,2},{2,3},{3,4},{4,5},{5,6},{6,7},{7,8},{8,9},{9,10},{10,1... | collective-permute-start | bytes 331784 | tf_op jit(solution)/shard_map/ppermute | solution.py:577
  37.9 2.1 %collective-permute-start.13 = (bf16[432,128]{1,0:T(8,128)(2,1)S(1)}, bf16[432,128]{1,0:T(8,128)(2,1)S(1)}, u32[]{:S(2)}, u32[]{:S(2)}) collective-permute-start(bf16[432,128]{1,0:T(8,128)(2,1)S(1)} %get-tuple-element.79.refs_5_), channel_id=1, source_target_pairs={{0,31},{1,0},{2,1},{3,2},{4,3},{5,4},{6,5},{7,6},{8,7},{9,8},{10,9... | collective-permute-start | bytes 331784 | tf_op jit(solution)/shard_map/ppermute | solution.py:577
  40.0 3.3 %collective-permute-start.14 = (bf16[224,128]{1,0:T(8,128)(2,1)S(1)}, bf16[224,128]{1,0:T(8,128)(2,1)S(1)}, u32[]{:S(2)}, u32[]{:S(2)}) collective-permute-start(bf16[224,128]{1,0:T(8,128)(2,1)S(1)} %get-tuple-element.80), channel_id=1, source_target_pairs={{0,2},{1,3},{2,4},{3,5},{4,6},{5,7},{6,8},{7,9},{8,10},{9,11},{10,... | collective-permute-start | bytes 172040 | tf_op jit(solution)/shard_map/ppermute | solution.py:577
  43.3 0.0 collective-permute-start.15
  43.3 1.8 %collective-permute-done.14.refs_2_ = bf16[224,128]{1,0:T(8,128)(2,1)S(1)} collective-permute-done((bf16[224,128]{1,0:T(8,128)(2,1)S(1)}, bf16[224,128]{1,0:T(8,128)(2,1)S(1)}, u32[]{:S(2)}, u32[]{:S(2)}) %collective-permute-start.14) | collective-permute-done | bytes 57376 | tf_op jit(solution)/shard_map/ppermute | solution.py:577
  45.2 5.7 %collective-permute-done.15.refs_3_ = bf16[224,128]{1,0:T(8,128)(2,1)S(1)} collective-permute-done((bf16[224,128]{1,0:T(8,128)(2,1)S(1)}, bf16[224,128]{1,0:T(8,128)(2,1)S(1)}, u32[]{:S(2)}, u32[]{:S(2)}) %collective-permute-start.15) | collective-permute-done | bytes 57376 | tf_op jit(solution)/shard_map/ppermute | solution.py:577
  50.8 0.0 collective-permute-done.12.refs_0_
  50.8 0.0 collective-permute-done.13.refs_1_
  50.8 1.1 %second_join.1 = (bf16[1944,128]{1,0:T(8,128)(2,1)}, f32[9,1,128]{2,1,0:T(1,128)}) custom-call(f32[104,128]{1,0:T(8,128)S(1)} %get-tuple-element.44.shape_ref, bf16[432,128]{1,0:T(8,128)(2,1)S(1)} %collective-permute-done.12.refs_0_, bf16[432,128]{1,0:T(8,128)(2,1)S(1)} %collective-permute-done.13.refs_1_, ...), custom_call_target="tpu_custom_call" | custom-call | flops 10000000 | bytes 3000000 | tf_op jit(solution)/shard_map/second_join/pallas_call | solution.py:658
Async XLA Ops:
  2.9 13.3 %collective-permute-start.4 = (bf16[1056,128]{1,0:T(8,128)(2,1)S(1)}, bf16[1056,128]{1,0:T(8,128)(2,1)S(1)}, u32[]{:S(2)}, u32[]{:S(2)}) collective-permute-start(bf16[1056,128]{1,0:T(8,128)(2,1)S(1)} %get-tuple-element.55), channel_id=1, source_target_pairs={{0,32},{32,0},{64,96},{96,64},{1,33},{33,1},{65,97},{97,65},{2,34}... | collective-permute-start | bytes 811016 | tf_op jit(solution)/shard_map/ppermute | solution.py:581
  3.0 6.5 %collective-permute-start = (bf16[528,128]{1,0:T(8,128)(2,1)S(1)}, bf16[528,128]{1,0:T(8,128)(2,1)S(1)}, u32[]{:S(2)}, u32[]{:S(2)}) collective-permute-start(bf16[528,128]{1,0:T(8,128)(2,1)S(1)} %get-tuple-element.50), channel_id=1, source_target_pairs={{0,64},{32,96},{64,0},{96,32},{1,65},{33,97},{65,1},{97,33},{2,66}... | collective-permute-start | bytes 405512 | tf_op jit(solution)/shard_map/ppermute | solution.py:581
  5.0 6.8 %collective-permute-start.1 = (bf16[528,128]{1,0:T(8,128)(2,1)S(1)}, bf16[528,128]{1,0:T(8,128)(2,1)S(1)}, u32[]{:S(2)}, u32[]{:S(2)}) collective-permute-start(bf16[528,128]{1,0:T(8,128)(2,1)S(1)} %get-tuple-element.51), channel_id=1, source_target_pairs={{0,96},{32,64},{64,32},{96,0},{1,97},{33,65},{65,33},{97,1},{2,98}... | collective-permute-start | bytes 405512 | tf_op jit(solution)/shard_map/ppermute | solution.py:581
  5.0 12.5 %collective-permute-start.5 = (bf16[528,128]{1,0:T(8,128)(2,1)S(1)}, bf16[528,128]{1,0:T(8,128)(2,1)S(1)}, u32[]{:S(2)}, u32[]{:S(2)}) collective-permute-start(bf16[528,128]{1,0:T(8,128)(2,1)S(1)} %get-tuple-element.56), channel_id=1, source_target_pairs={{0,64},{32,96},{64,0},{96,32},{1,65},{33,97},{65,1},{97,33},{2,66}... | collective-permute-start | bytes 405512 | tf_op jit(solution)/shard_map/ppermute | solution.py:581
  6.8 10.8 %collective-permute-start.6 = (bf16[528,128]{1,0:T(8,128)(2,1)S(1)}, bf16[528,128]{1,0:T(8,128)(2,1)S(1)}, u32[]{:S(2)}, u32[]{:S(2)}) collective-permute-start(bf16[528,128]{1,0:T(8,128)(2,1)S(1)} %get-tuple-element.57), channel_id=1, source_target_pairs={{0,96},{32,64},{64,32},{96,0},{1,97},{33,65},{65,33},{97,1},{2,98}... | collective-permute-start | bytes 405512 | tf_op jit(solution)/shard_map/ppermute | solution.py:581
  11.8 10.5 %collective-permute-start.2 = (bf16[448,128]{1,0:T(8,128)(2,1)S(1)}, bf16[448,128]{1,0:T(8,128)(2,1)S(1)}, u32[]{:S(2)}, u32[]{:S(2)}) collective-permute-start(bf16[448,128]{1,0:T(8,128)(2,1)S(1)} %get-tuple-element.52.refs_4_), channel_id=1, source_target_pairs={{0,1},{1,2},{2,3},{3,4},{4,5},{5,6},{6,7},{7,8},{8,9},{9,10},{10,1... | collective-permute-start | bytes 344072 | tf_op jit(solution)/shard_map/ppermute | solution.py:577
  15.3 10.7 %collective-permute-start.3 = (bf16[448,128]{1,0:T(8,128)(2,1)S(1)}, bf16[448,128]{1,0:T(8,128)(2,1)S(1)}, u32[]{:S(2)}, u32[]{:S(2)}) collective-permute-start(bf16[448,128]{1,0:T(8,128)(2,1)S(1)} %get-tuple-element.53.refs_5_), channel_id=1, source_target_pairs={{0,31},{1,0},{2,1},{3,2},{4,3},{5,4},{6,5},{7,6},{8,7},{9,8},{10,9... | collective-permute-start | bytes 344072 | tf_op jit(solution)/shard_map/ppermute | solution.py:577
  19.8 14.1 %collective-permute-start.10 = (bf16[528,128]{1,0:T(8,128)(2,1)S(1)}, bf16[528,128]{1,0:T(8,128)(2,1)S(1)}, u32[]{:S(2)}, u32[]{:S(2)}) collective-permute-start(bf16[528,128]{1,0:T(8,128)(2,1)S(1)} %get-tuple-element.76), channel_id=1, source_target_pairs={{0,64},{32,96},{64,0},{96,32},{1,65},{33,97},{65,1},{97,33},{2,66}... | collective-permute-start | bytes 405512 | tf_op jit(solution)/shard_map/ppermute | solution.py:581
  21.4 12.5 %collective-permute-start.11 = (bf16[528,128]{1,0:T(8,128)(2,1)S(1)}, bf16[528,128]{1,0:T(8,128)(2,1)S(1)}, u32[]{:S(2)}, u32[]{:S(2)}) collective-permute-start(bf16[528,128]{1,0:T(8,128)(2,1)S(1)} %get-tuple-element.77), channel_id=1, source_target_pairs={{0,96},{32,64},{64,32},{96,0},{1,97},{33,65},{65,33},{97,1},{2,98}... | collective-permute-start | bytes 405512 | tf_op jit(solution)/shard_map/ppermute | solution.py:581
  22.2 11.7 %collective-permute-start.9 = (bf16[528,128]{1,0:T(8,128)(2,1)S(1)}, bf16[528,128]{1,0:T(8,128)(2,1)S(1)}, u32[]{:S(2)}, u32[]{:S(2)}) collective-permute-start(bf16[528,128]{1,0:T(8,128)(2,1)S(1)} %get-tuple-element.75), channel_id=1, source_target_pairs={{0,32},{32,0},{64,96},{96,64},{1,33},{33,1},{65,97},{97,65},{2,34}... | collective-permute-start | bytes 405512 | tf_op jit(solution)/shard_map/ppermute | solution.py:581
  26.0 4.2 %collective-permute-start.7 = (bf16[224,128]{1,0:T(8,128)(2,1)S(1)}, bf16[224,128]{1,0:T(8,128)(2,1)S(1)}, u32[]{:S(2)}, u32[]{:S(2)}) collective-permute-start(bf16[224,128]{1,0:T(8,128)(2,1)S(1)} %get-tuple-element.70), channel_id=1, source_target_pairs={{0,2},{1,3},{2,4},{3,5},{4,6},{5,7},{6,8},{7,9},{8,10},{9,11},{10,... | collective-permute-start | bytes 172040 | tf_op jit(solution)/shard_map/ppermute | solution.py:577
  26.2 7.5 %collective-permute-start.8 = (bf16[224,128]{1,0:T(8,128)(2,1)S(1)}, bf16[224,128]{1,0:T(8,128)(2,1)S(1)}, u32[]{:S(2)}, u32[]{:S(2)}) collective-permute-start(bf16[224,128]{1,0:T(8,128)(2,1)S(1)} %get-tuple-element.71), channel_id=1, source_target_pairs={{0,30},{1,31},{2,0},{3,1},{4,2},{5,3},{6,4},{7,5},{8,6},{9,7},{10,... | collective-permute-start | bytes 172040 | tf_op jit(solution)/shard_map/ppermute | solution.py:577
  35.5 15.3 %collective-permute-start.12 = (bf16[432,128]{1,0:T(8,128)(2,1)S(1)}, bf16[432,128]{1,0:T(8,128)(2,1)S(1)}, u32[]{:S(2)}, u32[]{:S(2)}) collective-permute-start(bf16[432,128]{1,0:T(8,128)(2,1)S(1)} %get-tuple-element.78.refs_4_), channel_id=1, source_target_pairs={{0,1},{1,2},{2,3},{3,4},{4,5},{5,6},{6,7},{7,8},{8,9},{9,10},{10,1... | collective-permute-start | bytes 331784 | tf_op jit(solution)/shard_map/ppermute | solution.py:577
  37.9 12.9 %collective-permute-start.13 = (bf16[432,128]{1,0:T(8,128)(2,1)S(1)}, bf16[432,128]{1,0:T(8,128)(2,1)S(1)}, u32[]{:S(2)}, u32[]{:S(2)}) collective-permute-start(bf16[432,128]{1,0:T(8,128)(2,1)S(1)} %get-tuple-element.79.refs_5_), channel_id=1, source_target_pairs={{0,31},{1,0},{2,1},{3,2},{4,3},{5,4},{6,5},{7,6},{8,7},{9,8},{10,9... | collective-permute-start | bytes 331784 | tf_op jit(solution)/shard_map/ppermute | solution.py:577
  40.0 5.2 %collective-permute-start.14 = (bf16[224,128]{1,0:T(8,128)(2,1)S(1)}, bf16[224,128]{1,0:T(8,128)(2,1)S(1)}, u32[]{:S(2)}, u32[]{:S(2)}) collective-permute-start(bf16[224,128]{1,0:T(8,128)(2,1)S(1)} %get-tuple-element.80), channel_id=1, source_target_pairs={{0,2},{1,3},{2,4},{3,5},{4,6},{5,7},{6,8},{7,9},{8,10},{9,11},{10,... | collective-permute-start | bytes 172040 | tf_op jit(solution)/shard_map/ppermute | solution.py:577
  43.3 7.5 %collective-permute-start.15 = (bf16[224,128]{1,0:T(8,128)(2,1)S(1)}, bf16[224,128]{1,0:T(8,128)(2,1)S(1)}, u32[]{:S(2)}, u32[]{:S(2)}) collective-permute-start(bf16[224,128]{1,0:T(8,128)(2,1)S(1)} %get-tuple-element.81), channel_id=1, source_target_pairs={{0,30},{1,31},{2,0},{3,1},{4,2},{5,3},{6,4},{7,5},{8,6},{9,7},{10,... | collective-permute-start | bytes 172040 | tf_op jit(solution)/shard_map/ppermute | solution.py:577

commit v3 on v2

--- a/solution.py
+++ b/solution.py
@@ -256,12 +256,8 @@
         return jnp.concatenate([ref[pos ^ flip] for flip in range(4)], axis=1)
 
     analysis = pick(an_ref)
-    total = force[...]
-    high = total.astype(BF16)
-    low = (total - high.astype(F32)).astype(BF16)
-    result = (
-        jnp.dot(high, analysis, preferred_element_type=F32)
-        + jnp.dot(low, analysis, preferred_element_type=F32)
+    result = jnp.dot(
+        force[...].astype(BF16), analysis, preferred_element_type=F32
     ).astype(BF16)
     for flip, out in enumerate(outs):
         out[...] = result[:, 128 * flip : 128 * (flip + 1)]

time: 52.1 us -> 52.1 us (level)
  transfers between devices with their start and end apart: 16 -> 16, of which waited for: 7 -> 7; matrix products, arithmetic and copies ran while one was open for 0% -> 0% of each run, Pallas kernels for 10% -> 9%
where the time goes in v3:
time: 52.1 us; the launch traced here: 51.9 us
  waiting for transfers between devices  20.9 us (40%)
  starting transfers between devices  20.6 us (40%)
  Pallas kernels  9 us (17%)
  between operations  1.37 us (3%)
    ppermute x8, waiting for transfers between devices, ring(): lax.ppermute(value, 'xsec', [(n, (n + shift) % count) for n in range(coun...  17.4 us
    ppermute x8, starting transfers between devices, ring(): lax.ppermute(value, 'xsec', [(n, (n + shift) % count) for n in range(coun...  14.3 us
    ppermute x8, starting transfers between devices, swap(): lax.ppermute(value, 'span', [(n, n ^ flip) for n in range(lax.axis_size('...  6.28 us
    ppermute x8, waiting for transfers between devices, swap(): lax.ppermute(value, 'span', [(n, n ^ flip) for n in range(lax.axis_size('...  3.57 us
    pallas_call x1, Pallas kernels, forcing(): call(force_kernel, 'adjoint_forcing', [((ROWS, 128), BF16)] * 4, [pltpu.V...  1.82 us
    pallas_call x1, Pallas kernels, repack(): call(repack_kernel, 'span_groups', [((2 * ROWS, 128), BF16)] * 2 + [((ROW...  1.58 us
    pallas_call x1, Pallas kernels, local(): call(second_kernel, 'second_substep', [state_shape] + [((16 * COLS, 128),...  1.57 us
    pallas_call x1, Pallas kernels, local(): call(first_kernel, 'first_substep', [state_shape] + [((16 * COLS + 16, 12...  1.47 us
  transfers between devices with their start and end apart: 16, of which 7 were waited for; matrix products, arithmetic and copies ran while one was open for 0% of the time, Pallas kernels for 9%

profile of v3, /device:TPU:30, one launch (start us, length us, event | category | flops | bytes accessed | tf_op | source)
XLA Modules:
  0.0 51.9 jit_solution(10438568432027795337)
XLA Ops:
  1.3 1.6 %span_groups.1 = (bf16[1056,128]{1,0:T(8,128)(2,1)S(1)}, bf16[1056,128]{1,0:T(8,128)(2,1)S(1)}, bf16[528,128]{1,0:T(8,128)(2,1)S(1)}, bf16[528,128]{1,0:T(8,128)...) custom-call(s32[1]{0:T(128)} %bitcast.pos_ref, ...), custom_call_target="tpu_custom_call" | custom-call | flops 1000000 | bytes 2000000 | tf_op jit(solution)/shard_map/span_groups/pallas_call | solution.py:165
  2.9 0.1 collective-permute-start.4
  3.0 2.0 %collective-permute-start = (bf16[528,128]{1,0:T(8,128)(2,1)S(1)}, bf16[528,128]{1,0:T(8,128)(2,1)S(1)}, u32[]{:S(2)}, u32[]{:S(2)}) collective-permute-start(bf16[528,128]{1,0:T(8,128)(2,1)S(1)} %get-tuple-element.50), channel_id=1, source_target_pairs={{0,64},{32,96},{64,0},{96,32},{1,65},{33,97},{65,1},{97,33},{2,66}... | collective-permute-start | bytes 405512 | tf_op jit(solution)/shard_map/ppermute | solution.py:577
  5.0 0.1 collective-permute-start.1
  5.0 1.7 %collective-permute-start.5 = (bf16[528,128]{1,0:T(8,128)(2,1)S(1)}, bf16[528,128]{1,0:T(8,128)(2,1)S(1)}, u32[]{:S(2)}, u32[]{:S(2)}) collective-permute-start(bf16[528,128]{1,0:T(8,128)(2,1)S(1)} %get-tuple-element.56), channel_id=1, source_target_pairs={{0,64},{32,96},{64,0},{96,32},{1,65},{33,97},{65,1},{97,33},{2,66}... | collective-permute-start | bytes 405512 | tf_op jit(solution)/shard_map/ppermute | solution.py:577
  6.8 0.0 collective-permute-start.6
  6.8 1.5 %first_substep.1 = (f32[1944,128]{1,0:T(8,128)S(1)}, bf16[448,128]{1,0:T(8,128)(2,1)S(1)}, bf16[448,128]{1,0:T(8,128)(2,1)S(1)}, bf16[224,128]{1,0:T(8,128)(2,1)...) custom-call(s32[1]{0:T(128)} %bitcast.pos_ref, ...), custom_call_target="tpu_custom_call" | custom-call | flops 50000000 | bytes 3000000 | tf_op jit(solution)/shard_map/first_substep/pallas_call | solution.py:607
  8.2 1.2 %collective-permute-done.refs_2_ = bf16[528,128]{1,0:T(8,128)(2,1)S(1)} collective-permute-done((bf16[528,128]{1,0:T(8,128)(2,1)S(1)}, bf16[528,128]{1,0:T(8,128)(2,1)S(1)}, u32[]{:S(2)}, u32[]{:S(2)}) %collective-permute-start) | collective-permute-done | bytes 135200 | tf_op jit(solution)/shard_map/ppermute | solution.py:577
  9.4 2.4 %collective-permute-done.1.refs_3_ = bf16[528,128]{1,0:T(8,128)(2,1)S(1)} collective-permute-done((bf16[528,128]{1,0:T(8,128)(2,1)S(1)}, bf16[528,128]{1,0:T(8,128)(2,1)S(1)}, u32[]{:S(2)}, u32[]{:S(2)}) %collective-permute-start.1) | collective-permute-done | bytes 135200 | tf_op jit(solution)/shard_map/ppermute | solution.py:577
  11.8 3.6 %collective-permute-start.2 = (bf16[448,128]{1,0:T(8,128)(2,1)S(1)}, bf16[448,128]{1,0:T(8,128)(2,1)S(1)}, u32[]{:S(2)}, u32[]{:S(2)}) collective-permute-start(bf16[448,128]{1,0:T(8,128)(2,1)S(1)} %get-tuple-element.52.refs_4_), channel_id=1, source_target_pairs={{0,1},{1,2},{2,3},{3,4},{4,5},{5,6},{6,7},{7,8},{8,9},{9,10},{10,1... | collective-permute-start | bytes 344072 | tf_op jit(solution)/shard_map/ppermute | solution.py:573
  15.3 0.9 %collective-permute-start.3 = (bf16[448,128]{1,0:T(8,128)(2,1)S(1)}, bf16[448,128]{1,0:T(8,128)(2,1)S(1)}, u32[]{:S(2)}, u32[]{:S(2)}) collective-permute-start(bf16[448,128]{1,0:T(8,128)(2,1)S(1)} %get-tuple-element.53.refs_5_), channel_id=1, source_target_pairs={{0,31},{1,0},{2,1},{3,2},{4,3},{5,4},{6,5},{7,6},{8,7},{9,8},{10,9... | collective-permute-start | bytes 344072 | tf_op jit(solution)/shard_map/ppermute | solution.py:573
  16.2 0.0 collective-permute-done.4.refs_1_
  16.2 1.3 %adjoint_planes.1 = (f32[528,512]{1,0:T(8,128)S(1)}, f32[528,512]{1,0:T(8,128)S(1)}, f32[3,352,512]{2,1,0:T(8,128)S(1)}) custom-call(s32[1]{0:T(128)} %bitcast.pos_ref, bf16[1056,128]{1,0:T(8,128)(2,1)S(1)} %get-tuple-element.54.refs_0_, bf16[1056,128]{1,0:T(8,128)(2,1)S(1)} %collective-permute-done.4.refs_1_, ...), custom_call_target="tpu_custom_call" | custom-call | flops 1500000000 | bytes 8000000 | tf_op jit(solution)/shard_map/adjoint_planes/pallas_call | solution.py:271
  17.5 0.0 collective-permute-done.5.refs_2_
  17.5 0.0 collective-permute-done.6.refs_3_
  17.6 1.8 %adjoint_forcing.1 = (bf16[528,128]{1,0:T(8,128)(2,1)S(1)}, bf16[528,128]{1,0:T(8,128)(2,1)S(1)}, bf16[528,128]{1,0:T(8,128)(2,1)S(1)}, bf16[528,128]{1,0:T(8,128)(2,1)S(1)}) custom-call(s32[1]{0:T(128)} %bitcast.pos_ref, f32[104,128]{1,0:T(8,128)S(1)} %get-tuple-element.44.shape_ref, bf16[1056,128]{1,0:T(8,128)(2,1)S(1)} %get-tuple-element.54.refs_0_, ...), custom_call_target="tpu_custom_call" | custom-call | flops 2500000000 | bytes 8000000 | tf_op jit(solution)/shard_map/adjoint_forcing/pallas_call | solution.py:284
  19.4 1.6 %collective-permute-start.10 = (bf16[528,128]{1,0:T(8,128)(2,1)S(1)}, bf16[528,128]{1,0:T(8,128)(2,1)S(1)}, u32[]{:S(2)}, u32[]{:S(2)}) collective-permute-start(bf16[528,128]{1,0:T(8,128)(2,1)S(1)} %get-tuple-element.76), channel_id=1, source_target_pairs={{0,64},{32,96},{64,0},{96,32},{1,65},{33,97},{65,1},{97,33},{2,66}... | collective-permute-start | bytes 405512 | tf_op jit(solution)/shard_map/ppermute | solution.py:577
  21.0 0.8 %collective-permute-start.11 = (bf16[528,128]{1,0:T(8,128)(2,1)S(1)}, bf16[528,128]{1,0:T(8,128)(2,1)S(1)}, u32[]{:S(2)}, u32[]{:S(2)}) collective-permute-start(bf16[528,128]{1,0:T(8,128)(2,1)S(1)} %get-tuple-element.77), channel_id=1, source_target_pairs={{0,96},{32,64},{64,32},{96,0},{1,97},{33,65},{65,33},{97,1},{2,98}... | collective-permute-start | bytes 405512 | tf_op jit(solution)/shard_map/ppermute | solution.py:577
  21.8 0.0 collective-permute-start.9
  21.8 0.0 collective-permute-done.2.refs_0_
  21.8 4.3 %collective-permute-done.3.refs_1_ = bf16[448,128]{1,0:T(8,128)(2,1)S(1)} collective-permute-done((bf16[448,128]{1,0:T(8,128)(2,1)S(1)}, bf16[448,128]{1,0:T(8,128)(2,1)S(1)}, u32[]{:S(2)}, u32[]{:S(2)}) %collective-permute-start.3) | collective-permute-done | bytes 114720 | tf_op jit(solution)/shard_map/ppermute | solution.py:573
  26.0 0.1 collective-permute-start.7
  26.2 1.9 %collective-permute-start.8 = (bf16[224,128]{1,0:T(8,128)(2,1)S(1)}, bf16[224,128]{1,0:T(8,128)(2,1)S(1)}, u32[]{:S(2)}, u32[]{:S(2)}) collective-permute-start(bf16[224,128]{1,0:T(8,128)(2,1)S(1)} %get-tuple-element.71), channel_id=1, source_target_pairs={{0,30},{1,31},{2,0},{3,1},{4,2},{5,3},{6,4},{7,5},{8,6},{9,7},{10,... | collective-permute-start | bytes 172040 | tf_op jit(solution)/shard_map/ppermute | solution.py:573
  28.1 2.2 %collective-permute-done.7.refs_2_ = bf16[224,128]{1,0:T(8,128)(2,1)S(1)} collective-permute-done((bf16[224,128]{1,0:T(8,128)(2,1)S(1)}, bf16[224,128]{1,0:T(8,128)(2,1)S(1)}, u32[]{:S(2)}, u32[]{:S(2)}) %collective-permute-start.7) | collective-permute-done | bytes 57376 | tf_op jit(solution)/shard_map/ppermute | solution.py:573
  30.2 3.5 %collective-permute-done.8.refs_3_ = bf16[224,128]{1,0:T(8,128)(2,1)S(1)} collective-permute-done((bf16[224,128]{1,0:T(8,128)(2,1)S(1)}, bf16[224,128]{1,0:T(8,128)(2,1)S(1)}, u32[]{:S(2)}, u32[]{:S(2)}) %collective-permute-start.8) | collective-permute-done | bytes 57376 | tf_op jit(solution)/shard_map/ppermute | solution.py:573
  33.7 0.2 first_join.1
  33.9 0.0 collective-permute-done.10.refs_2_
  33.9 0.0 collective-permute-done.11.refs_3_
  33.9 0.0 collective-permute-done.9.refs_1_
  33.9 1.6 %second_substep.1 = (f32[1944,128]{1,0:T(8,128)S(1)}, bf16[432,128]{1,0:T(8,128)(2,1)S(1)}, bf16[432,128]{1,0:T(8,128)(2,1)S(1)}, bf16[224,128]{1,0:T(8,128)(2,1)S(1)}, bf16[224,128]{1,0:T(8,128)(2,1)S(1)}) custom-call(s32[1]{0:T(128)} %bitcast.pos_ref, f32[104,128]{1,0:T(8,128)S(1)} %get-tuple-element.44.shape_ref, ...), custom_call_target="tpu_custom_call" | custom-call | flops 50000000 | bytes 4000000 | tf_op jit(solution)/shard_map/second_substep/pallas_call | solution.py:642
  35.5 2.0 %collective-permute-start.12 = (bf16[432,128]{1,0:T(8,128)(2,1)S(1)}, bf16[432,128]{1,0:T(8,128)(2,1)S(1)}, u32[]{:S(2)}, u32[]{:S(2)}) collective-permute-start(bf16[432,128]{1,0:T(8,128)(2,1)S(1)} %get-tuple-element.78.refs_4_), channel_id=1, source_target_pairs={{0,1},{1,2},{2,3},{3,4},{4,5},{5,6},{6,7},{7,8},{8,9},{9,10},{10,1... | collective-permute-start | bytes 331784 | tf_op jit(solution)/shard_map/ppermute | solution.py:573
  37.5 2.5 %collective-permute-start.13 = (bf16[432,128]{1,0:T(8,128)(2,1)S(1)}, bf16[432,128]{1,0:T(8,128)(2,1)S(1)}, u32[]{:S(2)}, u32[]{:S(2)}) collective-permute-start(bf16[432,128]{1,0:T(8,128)(2,1)S(1)} %get-tuple-element.79.refs_5_), channel_id=1, source_target_pairs={{0,31},{1,0},{2,1},{3,2},{4,3},{5,4},{6,5},{7,6},{8,7},{9,8},{10,9... | collective-permute-start | bytes 331784 | tf_op jit(solution)/shard_map/ppermute | solution.py:573
  40.0 3.3 %collective-permute-start.14 = (bf16[224,128]{1,0:T(8,128)(2,1)S(1)}, bf16[224,128]{1,0:T(8,128)(2,1)S(1)}, u32[]{:S(2)}, u32[]{:S(2)}) collective-permute-start(bf16[224,128]{1,0:T(8,128)(2,1)S(1)} %get-tuple-element.80), channel_id=1, source_target_pairs={{0,2},{1,3},{2,4},{3,5},{4,6},{5,7},{6,8},{7,9},{8,10},{9,11},{10,... | collective-permute-start | bytes 172040 | tf_op jit(solution)/shard_map/ppermute | solution.py:573
  43.3 0.0 collective-permute-start.15
  43.3 1.8 %collective-permute-done.14.refs_2_ = bf16[224,128]{1,0:T(8,128)(2,1)S(1)} collective-permute-done((bf16[224,128]{1,0:T(8,128)(2,1)S(1)}, bf16[224,128]{1,0:T(8,128)(2,1)S(1)}, u32[]{:S(2)}, u32[]{:S(2)}) %collective-permute-start.14) | collective-permute-done | bytes 57376 | tf_op jit(solution)/shard_map/ppermute | solution.py:573
  45.2 5.7 %collective-permute-done.15.refs_3_ = bf16[224,128]{1,0:T(8,128)(2,1)S(1)} collective-permute-done((bf16[224,128]{1,0:T(8,128)(2,1)S(1)}, bf16[224,128]{1,0:T(8,128)(2,1)S(1)}, u32[]{:S(2)}, u32[]{:S(2)}) %collective-permute-start.15) | collective-permute-done | bytes 57376 | tf_op jit(solution)/shard_map/ppermute | solution.py:573
  50.8 0.0 collective-permute-done.12.refs_0_
  50.8 0.0 collective-permute-done.13.refs_1_
  50.8 1.1 %second_join.1 = (bf16[1944,128]{1,0:T(8,128)(2,1)}, f32[9,1,128]{2,1,0:T(1,128)}) custom-call(f32[104,128]{1,0:T(8,128)S(1)} %get-tuple-element.44.shape_ref, bf16[432,128]{1,0:T(8,128)(2,1)S(1)} %collective-permute-done.12.refs_0_, bf16[432,128]{1,0:T(8,128)(2,1)S(1)} %collective-permute-done.13.refs_1_, ...), custom_call_target="tpu_custom_call" | custom-call | flops 10000000 | bytes 3000000 | tf_op jit(solution)/shard_map/second_join/pallas_call | solution.py:654
Async XLA Ops:
  2.9 13.3 %collective-permute-start.4 = (bf16[1056,128]{1,0:T(8,128)(2,1)S(1)}, bf16[1056,128]{1,0:T(8,128)(2,1)S(1)}, u32[]{:S(2)}, u32[]{:S(2)}) collective-permute-start(bf16[1056,128]{1,0:T(8,128)(2,1)S(1)} %get-tuple-element.55), channel_id=1, source_target_pairs={{0,32},{32,0},{64,96},{96,64},{1,33},{33,1},{65,97},{97,65},{2,34}... | collective-permute-start | bytes 811016 | tf_op jit(solution)/shard_map/ppermute | solution.py:577
  3.0 6.5 %collective-permute-start = (bf16[528,128]{1,0:T(8,128)(2,1)S(1)}, bf16[528,128]{1,0:T(8,128)(2,1)S(1)}, u32[]{:S(2)}, u32[]{:S(2)}) collective-permute-start(bf16[528,128]{1,0:T(8,128)(2,1)S(1)} %get-tuple-element.50), channel_id=1, source_target_pairs={{0,64},{32,96},{64,0},{96,32},{1,65},{33,97},{65,1},{97,33},{2,66}... | collective-permute-start | bytes 405512 | tf_op jit(solution)/shard_map/ppermute | solution.py:577
  5.0 6.8 %collective-permute-start.1 = (bf16[528,128]{1,0:T(8,128)(2,1)S(1)}, bf16[528,128]{1,0:T(8,128)(2,1)S(1)}, u32[]{:S(2)}, u32[]{:S(2)}) collective-permute-start(bf16[528,128]{1,0:T(8,128)(2,1)S(1)} %get-tuple-element.51), channel_id=1, source_target_pairs={{0,96},{32,64},{64,32},{96,0},{1,97},{33,65},{65,33},{97,1},{2,98}... | collective-permute-start | bytes 405512 | tf_op jit(solution)/shard_map/ppermute | solution.py:577
  5.0 12.5 %collective-permute-start.5 = (bf16[528,128]{1,0:T(8,128)(2,1)S(1)}, bf16[528,128]{1,0:T(8,128)(2,1)S(1)}, u32[]{:S(2)}, u32[]{:S(2)}) collective-permute-start(bf16[528,128]{1,0:T(8,128)(2,1)S(1)} %get-tuple-element.56), channel_id=1, source_target_pairs={{0,64},{32,96},{64,0},{96,32},{1,65},{33,97},{65,1},{97,33},{2,66}... | collective-permute-start | bytes 405512 | tf_op jit(solution)/shard_map/ppermute | solution.py:577
  6.8 10.8 %collective-permute-start.6 = (bf16[528,128]{1,0:T(8,128)(2,1)S(1)}, bf16[528,128]{1,0:T(8,128)(2,1)S(1)}, u32[]{:S(2)}, u32[]{:S(2)}) collective-permute-start(bf16[528,128]{1,0:T(8,128)(2,1)S(1)} %get-tuple-element.57), channel_id=1, source_target_pairs={{0,96},{32,64},{64,32},{96,0},{1,97},{33,65},{65,33},{97,1},{2,98}... | collective-permute-start | bytes 405512 | tf_op jit(solution)/shard_map/ppermute | solution.py:577
  11.8 10.0 %collective-permute-start.2 = (bf16[448,128]{1,0:T(8,128)(2,1)S(1)}, bf16[448,128]{1,0:T(8,128)(2,1)S(1)}, u32[]{:S(2)}, u32[]{:S(2)}) collective-permute-start(bf16[448,128]{1,0:T(8,128)(2,1)S(1)} %get-tuple-element.52.refs_4_), channel_id=1, source_target_pairs={{0,1},{1,2},{2,3},{3,4},{4,5},{5,6},{6,7},{7,8},{8,9},{9,10},{10,1... | collective-permute-start | bytes 344072 | tf_op jit(solution)/shard_map/ppermute | solution.py:573
  15.3 10.7 %collective-permute-start.3 = (bf16[448,128]{1,0:T(8,128)(2,1)S(1)}, bf16[448,128]{1,0:T(8,128)(2,1)S(1)}, u32[]{:S(2)}, u32[]{:S(2)}) collective-permute-start(bf16[448,128]{1,0:T(8,128)(2,1)S(1)} %get-tuple-element.53.refs_5_), channel_id=1, source_target_pairs={{0,31},{1,0},{2,1},{3,2},{4,3},{5,4},{6,5},{7,6},{8,7},{9,8},{10,9... | collective-permute-start | bytes 344072 | tf_op jit(solution)/shard_map/ppermute | solution.py:573
  19.4 14.5 %collective-permute-start.10 = (bf16[528,128]{1,0:T(8,128)(2,1)S(1)}, bf16[528,128]{1,0:T(8,128)(2,1)S(1)}, u32[]{:S(2)}, u32[]{:S(2)}) collective-permute-start(bf16[528,128]{1,0:T(8,128)(2,1)S(1)} %get-tuple-element.76), channel_id=1, source_target_pairs={{0,64},{32,96},{64,0},{96,32},{1,65},{33,97},{65,1},{97,33},{2,66}... | collective-permute-start | bytes 405512 | tf_op jit(solution)/shard_map/ppermute | solution.py:577
  21.0 12.9 %collective-permute-start.11 = (bf16[528,128]{1,0:T(8,128)(2,1)S(1)}, bf16[528,128]{1,0:T(8,128)(2,1)S(1)}, u32[]{:S(2)}, u32[]{:S(2)}) collective-permute-start(bf16[528,128]{1,0:T(8,128)(2,1)S(1)} %get-tuple-element.77), channel_id=1, source_target_pairs={{0,96},{32,64},{64,32},{96,0},{1,97},{33,65},{65,33},{97,1},{2,98}... | collective-permute-start | bytes 405512 | tf_op jit(solution)/shard_map/ppermute | solution.py:577
  21.8 12.2 %collective-permute-start.9 = (bf16[528,128]{1,0:T(8,128)(2,1)S(1)}, bf16[528,128]{1,0:T(8,128)(2,1)S(1)}, u32[]{:S(2)}, u32[]{:S(2)}) collective-permute-start(bf16[528,128]{1,0:T(8,128)(2,1)S(1)} %get-tuple-element.75), channel_id=1, source_target_pairs={{0,32},{32,0},{64,96},{96,64},{1,33},{33,1},{65,97},{97,65},{2,34}... | collective-permute-start | bytes 405512 | tf_op jit(solution)/shard_map/ppermute | solution.py:577
  26.0 4.2 %collective-permute-start.7 = (bf16[224,128]{1,0:T(8,128)(2,1)S(1)}, bf16[224,128]{1,0:T(8,128)(2,1)S(1)}, u32[]{:S(2)}, u32[]{:S(2)}) collective-permute-start(bf16[224,128]{1,0:T(8,128)(2,1)S(1)} %get-tuple-element.70), channel_id=1, source_target_pairs={{0,2},{1,3},{2,4},{3,5},{4,6},{5,7},{6,8},{7,9},{8,10},{9,11},{10,... | collective-permute-start | bytes 172040 | tf_op jit(solution)/shard_map/ppermute | solution.py:573
  26.2 7.5 %collective-permute-start.8 = (bf16[224,128]{1,0:T(8,128)(2,1)S(1)}, bf16[224,128]{1,0:T(8,128)(2,1)S(1)}, u32[]{:S(2)}, u32[]{:S(2)}) collective-permute-start(bf16[224,128]{1,0:T(8,128)(2,1)S(1)} %get-tuple-element.71), channel_id=1, source_target_pairs={{0,30},{1,31},{2,0},{3,1},{4,2},{5,3},{6,4},{7,5},{8,6},{9,7},{10,... | collective-permute-start | bytes 172040 | tf_op jit(solution)/shard_map/ppermute | solution.py:573
  35.5 15.3 %collective-permute-start.12 = (bf16[432,128]{1,0:T(8,128)(2,1)S(1)}, bf16[432,128]{1,0:T(8,128)(2,1)S(1)}, u32[]{:S(2)}, u32[]{:S(2)}) collective-permute-start(bf16[432,128]{1,0:T(8,128)(2,1)S(1)} %get-tuple-element.78.refs_4_), channel_id=1, source_target_pairs={{0,1},{1,2},{2,3},{3,4},{4,5},{5,6},{6,7},{7,8},{8,9},{9,10},{10,1... | collective-permute-start | bytes 331784 | tf_op jit(solution)/shard_map/ppermute | solution.py:573
  37.5 13.4 %collective-permute-start.13 = (bf16[432,128]{1,0:T(8,128)(2,1)S(1)}, bf16[432,128]{1,0:T(8,128)(2,1)S(1)}, u32[]{:S(2)}, u32[]{:S(2)}) collective-permute-start(bf16[432,128]{1,0:T(8,128)(2,1)S(1)} %get-tuple-element.79.refs_5_), channel_id=1, source_target_pairs={{0,31},{1,0},{2,1},{3,2},{4,3},{5,4},{6,5},{7,6},{8,7},{9,8},{10,9... | collective-permute-start | bytes 331784 | tf_op jit(solution)/shard_map/ppermute | solution.py:573
  40.0 5.2 %collective-permute-start.14 = (bf16[224,128]{1,0:T(8,128)(2,1)S(1)}, bf16[224,128]{1,0:T(8,128)(2,1)S(1)}, u32[]{:S(2)}, u32[]{:S(2)}) collective-permute-start(bf16[224,128]{1,0:T(8,128)(2,1)S(1)} %get-tuple-element.80), channel_id=1, source_target_pairs={{0,2},{1,3},{2,4},{3,5},{4,6},{5,7},{6,8},{7,9},{8,10},{9,11},{10,... | collective-permute-start | bytes 172040 | tf_op jit(solution)/shard_map/ppermute | solution.py:573
  43.3 7.5 %collective-permute-start.15 = (bf16[224,128]{1,0:T(8,128)(2,1)S(1)}, bf16[224,128]{1,0:T(8,128)(2,1)S(1)}, u32[]{:S(2)}, u32[]{:S(2)}) collective-permute-start(bf16[224,128]{1,0:T(8,128)(2,1)S(1)} %get-tuple-element.81), channel_id=1, source_target_pairs={{0,30},{1,31},{2,0},{3,1},{4,2},{5,3},{6,4},{7,5},{8,6},{9,7},{10,... | collective-permute-start | bytes 172040 | tf_op jit(solution)/shard_map/ppermute | solution.py:573
